TPU v7x, 32 devices: a whole 2x2x4 slice. The times are simulated.
32 devices in a mesh: group: 4 (over y, x), ep: 8 (over z, core).
Axes of the slice: x: 2, y: 2, z: 4, core: 2. Of those that a mesh axis runs over, the one named last changes fastest.
Arguments:
- hidden_in: bfloat16 [2, 64, 7168], P(None, 'ep'), may hold values from -6 to 6
- queries: bfloat16 [2, 64, 64, 576], P(None, 'ep', 'group'), may hold values from -60 to 60
- latent_cache: bfloat16 [2, 64, 256, 576], P(None, 'ep'), may hold values from -8 to 8
- cache_lengths: int32 [2, 64], P(None, 'ep'), may hold values from 1 to 256, as said below
- expert_ids: int32 [2, 64, 4], P(None, 'ep'), may hold values from 0 to 3, all different within a row; in each aligned block of 8 rows (0 to 7, 8 to 15, ..., all dimensions but the last counted through in order) at most 8 rows name the same one
- gate_values: float32 [2, 64, 4], P(None, 'ep'), may hold values from 0.1 to 1
- norm_gain: float32 [7168], replicated, may hold values from 0.1 to 1.9
- value_up: bfloat16 [64, 512, 128], P('group'), may hold values from -0.25 to 0.25
- out_proj: bfloat16 [8192, 7168], P('group', 'ep'), may hold values from -0.0625 to 0.0625
- gate_up: bfloat16 [8, 7168, 2, 512], P('ep', 'group'), may hold values from -0.0625 to 0.0625
- down_proj: bfloat16 [8, 512, 7168], P('ep', 'group'), may hold values from -0.1875 to 0.1875
Outputs:
- layer_out: bfloat16 [2, 64, 7168], P(None, 'ep')
Inputs may be any that keep to these rules, and one draw needn't show every extreme that they name: `expert_ids`: in each micro-batch no expert is named by more than 8 of the 8 rows of one ep index, a bound that some block reaches; a row names 4 different experts. `cache_lengths`: some row of every ep index holds 256 valid positions in each micro-batch.
All inputs are finite; a program needn't handle non-finite values.
Results may differ from a plain program's by a relative error of at most 0.015.
Values may be sent and summed in bfloat16 or wider, within the bound.
A program may use at most 128 MiB of HBM per device.

v0:
```python
import math

import jax
import jax.numpy as jnp
from jax import lax
from jax.sharding import PartitionSpec as P

ROPE = 64
NOPE = 128


def attend(queries, cache, lengths, value_up):
    row_count, head_count, key_width = queries.shape
    latent_width = value_up.shape[1]
    score_scale = 1.0 / math.sqrt(NOPE + ROPE)
    scores = (
        jnp.einsum("rhk,rlk->rhl", queries, cache, preferred_element_type=jnp.float32) * score_scale
    )
    in_range = jnp.arange(cache.shape[1], dtype=jnp.int32)[None, None, :] < lengths[:, None, None]
    masked = jnp.where(in_range, scores, -1e30)
    peak_score = jnp.max(masked, axis=2, keepdims=True)
    exponent = jnp.where(in_range, jnp.exp(masked - peak_score), 0.0)
    weights = (exponent / jnp.sum(exponent, axis=2, keepdims=True)).astype(jnp.bfloat16)
    latent = jnp.einsum(
        "rhl,rlc->rhc", weights, cache[:, :, :latent_width], preferred_element_type=jnp.float32
    ).astype(jnp.bfloat16)
    head_out = jnp.einsum(
        "rhc,hcv->rhv", latent, value_up, preferred_element_type=jnp.float32
    ).astype(jnp.bfloat16)
    return head_out.reshape(row_count, head_count * value_up.shape[2])


def rms_scale(residual, norm_gain):
    mean_square = jnp.mean(residual * residual, axis=1, keepdims=True)
    return (residual * lax.rsqrt(mean_square + 1e-06) * norm_gain[None, :]).astype(jnp.bfloat16)


def routing_tables(expert_ids, gate_values, expert_count, capacity):
    row_count, top_count = expert_ids.shape
    onehot = (
        expert_ids[:, :, None] == jnp.arange(expert_count, dtype=jnp.int32)[None, None, :]
    ).astype(jnp.int32)
    flat_hot = onehot.reshape(row_count * top_count, expert_count)
    before = jnp.cumsum(flat_hot, axis=0) - flat_hot
    slot_index = jnp.sum(before * flat_hot, axis=1).reshape(row_count, top_count)
    slot_hot = (
        slot_index[:, :, None] == jnp.arange(capacity, dtype=jnp.int32)[None, None, :]
    ).astype(jnp.float32)
    chosen = onehot.astype(jnp.float32)
    select = jnp.einsum("rke,rkc->ecr", chosen, slot_hot, precision=lax.Precision.HIGHEST)
    weighted = jnp.einsum(
        "rke,rkc,rk->ecr", chosen, slot_hot, gate_values, precision=lax.Precision.HIGHEST
    )
    return (select.astype(jnp.bfloat16), weighted)


def pack_rows(select, features):
    packed = jnp.einsum("ecr,rd->ecd", select, features, preferred_element_type=jnp.float32).astype(
        jnp.bfloat16
    )
    return jnp.repeat(packed, 2, axis=0)


def local(
    hidden_in,
    queries,
    latent_cache,
    cache_lengths,
    expert_ids,
    gate_values,
    norm_gain,
    value_up,
    out_proj,
    gate_up,
    down_proj,
):
    feature_count = hidden_in.shape[2]
    expert_count = lax.axis_size("ep") // 2
    row_local = hidden_in.shape[1]
    top_count = expert_ids.shape[2]
    capacity = min(row_local, 2 * row_local * top_count // expert_count)
    down_local = down_proj[0]
    moved = lax.all_to_all(gate_up, "group", split_axis=3, concat_axis=1, tiled=True)
    local_gate_up = moved[0].reshape(feature_count, -1)
    results = []
    for micro in range(hidden_in.shape[0]):
        head_values = attend(queries[micro], latent_cache[micro], cache_lengths[micro], value_up)
        spread = jnp.dot(
            lax.all_gather(head_values, "ep", axis=0, tiled=True),
            out_proj,
            preferred_element_type=jnp.float32,
        )
        own_rows = lax.all_to_all(spread, "ep", split_axis=0, concat_axis=1, tiled=True)
        attended = lax.psum(own_rows, "group")
        residual = hidden_in[micro].astype(jnp.float32) + attended
        normed = rms_scale(residual, norm_gain)
        select, weighted = routing_tables(
            expert_ids[micro], gate_values[micro], expert_count, capacity
        )
        outgoing = pack_rows(select, normed)
        received = lax.all_to_all(outgoing, "ep", split_axis=0, concat_axis=0, tiled=True)
        rollout_senders, rollout_item_count, width_in = received.shape
        rollout_pre_act = jnp.dot(
            received.reshape(rollout_senders * rollout_item_count, width_in),
            local_gate_up,
            preferred_element_type=jnp.float32,
        )
        pre_act = rollout_pre_act.reshape(rollout_senders * rollout_item_count, 2, -1)
        activation = (jax.nn.silu(pre_act[:, 0]) * pre_act[:, 1]).astype(jnp.bfloat16)
        block_part = jnp.dot(activation, down_local, preferred_element_type=jnp.float32).reshape(
            rollout_senders, rollout_item_count, feature_count
        )
        gathered = lax.all_to_all(
            block_part.astype(jnp.bfloat16), "ep", split_axis=0, concat_axis=0, tiled=True
        ).astype(block_part.dtype)
        gathered = gathered.reshape(expert_count, 2, capacity, -1)
        expert_mix = jnp.einsum("ecr,ehcd->rd", weighted, gathered, precision=lax.Precision.HIGHEST)
        expert_total = lax.psum(expert_mix.astype(jnp.bfloat16), "group").astype(jnp.float32)
        results.append((residual + expert_total).astype(jnp.bfloat16))
    return jnp.stack(results)


def solution(mesh):
    return jax.shard_map(
        local,
        mesh=mesh,
        in_specs=(
            P(None, "ep", None),
            P(None, "ep", "group", None),
            P(None, "ep", None, None),
            P(None, "ep"),
            P(None, "ep", None),
            P(None, "ep", None),
            P(),
            P("group", None, None),
            P("group", "ep"),
            P("ep", "group", None, None),
            P("ep", "group", None),
        ),
        out_specs=P(None, "ep", None),
        check_vma=False,
    )
```

profile of v0, /device:TPU:1, one launch (start us, length us, event | category | flops | bytes accessed | tf_op | source)
XLA Modules:
  0.0 336.8 jit_solution(7854339323182243515)
XLA Ops:
  6.5 5.3 %slice_bitcast_fusion = (bf16[8,256,576]{1,2,0:T(8,128)(2,1)}, bf16[8,256,576]{1,2,0:T(8,128)(2,1)}) fusion(bf16[2,8,256,576]{2,3,1,0:T(8,128)(2,1)} %param.13), kind=kLoop, calls=%fused_computation.10 | loop fusion | bytes 9437184 | tf_op jit(solution)/shard_map/squeeze | solution.py:87
  11.9 0.4 fusion.19
  12.3 0.2 fusion.93
  12.5 2.3 fusion.10
  14.8 0.4 fusion.25
  15.2 15.8 %all_gather.6 = bf16[64,2048]{1,0:T(8,128)(2,1)S(1)} all-gather(bf16[8,2048]{1,0:T(8,128)(2,1)S(1)} %fusion.25), channel_id=1, replica_groups=mesh['group'=4,'ep'=8] {'ep'}, dimensions={0}, use_global_device_ids=true | all-gather | bytes 294912 | tf_op jit(solution)/shard_map/all_gather | solution.py:89
  31.0 3.4 %convolution_bitcast_fusion.3 = f32[8,8,896]{2,1,0:T(8,128)} fusion(bf16[64,2048]{1,0:T(8,128)(2,1)S(1)} %all_gather.6, bf16[2048,896]{1,0:T(8,128)(2,1)} %param.19), kind=kOutput, calls=%fused_computation.21 | convolution fusion | flops 234881024 | bytes 4161536 | tf_op jit(solution)/shard_map/dot_general | solution.py:88
  34.4 4.8 %all-to-all-start = ((f32[8,8,896]{2,1,0:T(8,128)}), f32[8,8,896]{2,1,0:T(8,128)S(1)}, u32[]{:S(2)}, u32[]{:S(2)}) async-start(f32[8,8,896]{2,1,0:T(8,128)} %convolution_bitcast_fusion.3), calls=%async_computation | async-start | bytes 458752 | tf_op jit(solution)/shard_map/all_to_all | solution.py:93
  39.3 2.1 fusion.18
  41.4 0.2 fusion.94
  41.6 2.3 fusion.13
  43.8 0.4 fusion.24
  44.3 14.6 %all_gather.7 = bf16[64,2048]{1,0:T(8,128)(2,1)S(1)} all-gather(bf16[8,2048]{1,0:T(8,128)(2,1)S(1)} %fusion.24), channel_id=1, replica_groups=mesh['group'=4,'ep'=8] {'ep'}, dimensions={0}, use_global_device_ids=true | all-gather | bytes 294912 | tf_op jit(solution)/shard_map/all_gather | solution.py:89
  58.9 3.5 %convolution_bitcast_fusion.2 = f32[8,8,896]{2,1,0:T(8,128)} fusion(bf16[64,2048]{1,0:T(8,128)(2,1)S(1)} %all_gather.7, bf16[2048,896]{1,0:T(8,128)(2,1)} %param.19), kind=kOutput, calls=%fused_computation.20 | convolution fusion | flops 234881024 | bytes 4161536 | tf_op jit(solution)/shard_map/dot_general | solution.py:88
  62.3 4.7 %all-to-all-start.4 = ((f32[8,8,896]{2,1,0:T(8,128)}), f32[8,8,896]{2,1,0:T(8,128)S(1)}, u32[]{:S(2)}, u32[]{:S(2)}) async-start(f32[8,8,896]{2,1,0:T(8,128)} %convolution_bitcast_fusion.2), calls=%async_computation.4 | async-start | bytes 458752 | tf_op jit(solution)/shard_map/all_to_all | solution.py:93
  67.1 0.1 copy.55
  67.2 0.1 copy.53
  67.2 0.1 eq.90
  67.3 7.8 %all-to-all-done.4 = f32[8,8,896]{2,1,0:T(8,128)S(1)} async-done(((f32[8,8,896]{2,1,0:T(8,128)}), f32[8,8,896]{2,1,0:T(8,128)S(1)}, u32[]{:S(2)}, u32[]{:S(2)}) %all-to-all-start.4) | async-done | bytes 229408 | tf_op jit(solution)/shard_map/all_to_all | solution.py:93
  75.1 0.7 copy-done.9
  75.9 0.2 select_reduce_fusion
  76.1 0.1 eq.94
  76.2 0.2 fusion.27
  76.4 43.1 %all-reduce.5.cloned.1.call-done = (f32[8,7168]{1,0:T(8,128)}, f32[8,7168]{1,0:T(8,128)}) async-done(((f32[8,7168]{1,0:T(8,128)}, f32[8,7168]{1,0:T(8,128)}), (f32[8,7168]{1,0:T(8,128)}, f32[8,7168]{1,0:T(8,128)})) %all-reduce.5.cloned.1.call-update) | async-done | bytes 458768 | tf_op jit(solution)/shard_map/psum | solution.py:94
  119.6 1.2 multiply_reduce_fusion.1
  120.9 1.3 convolution_convert_fusion.2
  122.2 1.0 broadcast_in_dim.53
  123.1 5.7 %all-to-all-start.5 = ((bf16[8,8,7168]{2,1,0:T(8,128)(2,1)}), bf16[8,8,7168]{2,1,0:T(8,128)(2,1)S(1)}, u32[]{:S(2)}, u32[]{:S(2)}) async-start(bf16[8,8,7168]{2,1,0:T(8,128)(2,1)} %bitcast.41), calls=%async_computation.5 | async-start | bytes 1835008 | tf_op jit(solution)/shard_map/all_to_all | solution.py:101
  128.8 13.6 %copy.48 = bf16[1,1792,2,512]{1,2,0,3:T(2,128)(2,1)} copy(bf16[1,1792,2,512]{3,2,1,0:T(2,128)(2,1)} %param.20) | data formatting | bytes 7340032 | tf_op args[9]
  142.5 9.3 %all-to-all-done.5 = bf16[8,8,7168]{2,1,0:T(8,128)(2,1)S(1)} async-done(((bf16[8,8,7168]{2,1,0:T(8,128)(2,1)}), bf16[8,8,7168]{2,1,0:T(8,128)(2,1)S(1)}, u32[]{:S(2)}, u32[]{:S(2)}) %all-to-all-start.5) | async-done | bytes 917536 | tf_op jit(solution)/shard_map/all_to_all | solution.py:101
  151.8 4.7 %all-to-all-start.2 = ((bf16[1,1792,2,512]{1,2,0,3:T(2,128)(2,1)}), bf16[1,1792,2,512]{1,2,0,3:T(2,128)(2,1)}, u32[]{:S(2)}, u32[]{:S(2)}) async-start(bf16[1,1792,2,512]{1,2,0,3:T(2,128)(2,1)} %copy.48), calls=%async_computation.2 | async-start | bytes 7340032 | tf_op jit(solution)/shard_map/all_to_all | solution.py:83
  156.5 0.1 copy.46
  156.6 0.1 copy.44
  156.7 0.1 eq.78
  156.9 0.2 select_reduce_fusion.1
  157.1 0.1 eq.82
  157.2 0.2 fusion.26
  157.4 1.1 convolution_convert_fusion.3
  158.5 39.2 %all-to-all-done.2 = bf16[1,1792,2,512]{1,2,0,3:T(2,128)(2,1)} async-done(((bf16[1,1792,2,512]{1,2,0,3:T(2,128)(2,1)}), bf16[1,1792,2,512]{1,2,0,3:T(2,128)(2,1)}, u32[]{:S(2)}, u32[]{:S(2)}) %all-to-all-start.2) | async-done | bytes 3670048 | tf_op jit(solution)/shard_map/all_to_all | solution.py:83
  197.8 2.0 broadcast_in_dim.51
  199.8 5.6 %all-to-all-start.1 = ((bf16[8,8,7168]{2,1,0:T(8,128)(2,1)}), bf16[8,8,7168]{2,1,0:T(8,128)(2,1)}, u32[]{:S(2)}, u32[]{:S(2)}) async-start(bf16[8,8,7168]{2,1,0:T(8,128)(2,1)} %bitcast.14), calls=%async_computation.1 | async-start | bytes 1835008 | tf_op jit(solution)/shard_map/all_to_all | solution.py:101
  205.4 4.9 %copy.49 = bf16[1,4,1792,2,128]{2,1,4,3,0:T(4,128)(2,1)S(1)} copy(bf16[1,4,1792,2,128]{2,3,4,1,0:T(2,128)(2,1)} %bitcast.18) | data formatting | bytes 7340032 | tf_op jit(solution)/shard_map/all_to_all | solution.py:83
  210.2 0.7 copy.60
  210.9 1.8 copy-done.1
  212.8 1.2 fusion.28
  214.0 1.4 convolution_convert_fusion
  215.4 13.0 %all-to-all-done.1 = bf16[8,8,7168]{2,1,0:T(8,128)(2,1)} async-done(((bf16[8,8,7168]{2,1,0:T(8,128)(2,1)}), bf16[8,8,7168]{2,1,0:T(8,128)(2,1)}, u32[]{:S(2)}, u32[]{:S(2)}) %all-to-all-start.1) | async-done | bytes 917536 | tf_op jit(solution)/shard_map/all_to_all | solution.py:101
  228.4 4.3 %all-to-all-start.6 = ((bf16[8,8,7168]{2,1,0:T(8,128)(2,1)}), bf16[8,8,7168]{2,1,0:T(8,128)(2,1)S(1)}, u32[]{:S(2)}, u32[]{:S(2)}) async-start(bf16[8,8,7168]{2,1,0:T(8,128)(2,1)} %convolution_convert_fusion), calls=%async_computation.6 | async-start | bytes 1835008 | tf_op jit(solution)/shard_map/all_to_all | solution.py:113
  232.7 3.7 %fusion.30 = f32[64,2,128]{2,0,1:T(8,128)S(1)} fusion(bf16[2,128,7168]{2,1,0:T(8,128)(2,1)} %bitcast.145, bf16[8,8,7168]{2,1,0:T(8,128)(2,1)} %all-to-all-done.1), kind=kOutput, calls=%fused_computation.46 | convolution fusion | flops 234881024 | bytes 4653056 | tf_op jit(solution)/shard_map/dot_general | solution.py:103
  236.4 1.3 convolution_convert_fusion.1
  237.8 17.9 %all-to-all-done.6 = bf16[8,8,7168]{2,1,0:T(8,128)(2,1)S(1)} async-done(((bf16[8,8,7168]{2,1,0:T(8,128)(2,1)}), bf16[8,8,7168]{2,1,0:T(8,128)(2,1)S(1)}, u32[]{:S(2)}, u32[]{:S(2)}) %all-to-all-start.6) | async-done | bytes 917536 | tf_op jit(solution)/shard_map/all_to_all | solution.py:113
  255.7 5.0 %all-to-all-start.3 = ((bf16[8,8,7168]{2,1,0:T(8,128)(2,1)}), bf16[8,8,7168]{2,1,0:T(8,128)(2,1)}, u32[]{:S(2)}, u32[]{:S(2)}) async-start(bf16[8,8,7168]{2,1,0:T(8,128)(2,1)} %convolution_convert_fusion.1), calls=%async_computation.3 | async-start | bytes 1835008 | tf_op jit(solution)/shard_map/all_to_all | solution.py:113
  260.7 0.1 copy.54
  260.8 0.1 copy.45
  260.8 0.3 convolution_bitcast_fusion.4
  261.1 0.3 convolution_bitcast_fusion.5
  261.4 0.1 convert_reduce_fusion
  261.5 2.4 fusion.3
  263.9 19.8 %all-to-all-done.3 = bf16[8,8,7168]{2,1,0:T(8,128)(2,1)} async-done(((bf16[8,8,7168]{2,1,0:T(8,128)(2,1)}), bf16[8,8,7168]{2,1,0:T(8,128)(2,1)}, u32[]{:S(2)}, u32[]{:S(2)}) %all-to-all-start.3) | async-done | bytes 917536 | tf_op jit(solution)/shard_map/all_to_all | solution.py:113
  283.7 1.4 convert_reduce_fusion.1
  285.1 2.4 fusion.2
  287.6 40.7 %all-reduce.7.cloned.1.call-done = (bf16[8,7168]{1,0:T(8,128)(2,1)}, bf16[8,7168]{1,0:T(8,128)(2,1)}) async-done(((bf16[8,7168]{1,0:T(8,128)(2,1)}, bf16[8,7168]{1,0:T(8,128)(2,1)}), (bf16[8,7168]{1,0:T(8,128)(2,1)}, bf16[8,7168]{1,0:T(8,128)(2,1)})) %all-reduce.7.cloned.1.call-update) | async-done | bytes 229392 | tf_op jit(solution)/shard_map/psum | solution.py:118
  328.2 1.0 fusion.40
  329.3 0.7 copy-done.15
  (45 shorter events, 0.5 us)
Async XLA Ops:
  6.5 8.3 %copy-start = (bf16[16,512,128]{2,1,0:T(8,128)(2,1)S(1)}, bf16[16,512,128]{2,1,0:T(8,128)(2,1)}, u32[]{:S(2)}) copy-start(bf16[16,512,128]{2,1,0:T(8,128)(2,1)} %param.18) | copy-start | bytes 6291460
  6.5 5.4 %copy-start.4 = (bf16[2,8,256,576]{2,3,1,0:T(8,128)(2,1)S(1)}, bf16[2,8,256,576]{2,3,1,0:T(8,128)(2,1)}, u32[]{:S(2)}) copy-start(bf16[2,8,256,576]{2,3,1,0:T(8,128)(2,1)} %param.13) | copy-start | bytes 14155780
  6.5 5.3 %copy-start.13 = (s32[2,8]{1,0:T(2,128)S(1)}, s32[2,8]{1,0:T(2,128)}, u32[]{:S(2)}) copy-start(s32[2,8]{1,0:T(2,128)} %param.14) | copy-start | bytes 196
  6.5 5.4 %copy-start.14 = (bf16[2,8,16,576]{3,2,1,0:T(8,128)(2,1)S(1)}, bf16[2,8,16,576]{3,2,1,0:T(8,128)(2,1)}, u32[]{:S(2)}) copy-start(bf16[2,8,16,576]{3,2,1,0:T(8,128)(2,1)} %param.12) | copy-start | bytes 884740
  34.4 27.9 %all-to-all-start = ((f32[8,8,896]{2,1,0:T(8,128)}), f32[8,8,896]{2,1,0:T(8,128)S(1)}, u32[]{:S(2)}, u32[]{:S(2)}) async-start(f32[8,8,896]{2,1,0:T(8,128)} %convolution_bitcast_fusion.3), calls=%async_computation | async-start | bytes 458752 | tf_op jit(solution)/shard_map/all_to_all | solution.py:93
  58.8 8.2 %copy-start.11 = (s32[2,8,4]{1,2,0:T(4,128)S(1)}, s32[2,8,4]{1,2,0:T(4,128)}, u32[]{:S(2)}) copy-start(s32[2,8,4]{1,2,0:T(4,128)} %param.15) | copy-start | bytes 772
  58.8 60.7 %copy-start.7 = (bf16[2,8,7168]{2,1,0:T(8,128)(2,1)S(1)}, bf16[2,8,7168]{2,1,0:T(8,128)(2,1)}, u32[]{:S(2)}) copy-start(bf16[2,8,7168]{2,1,0:T(8,128)(2,1)} %param.11) | copy-start | bytes 688132
  58.8 62.0 %copy-start.10 = (f32[7168]{0:T(1024)S(1)}, f32[7168]{0:T(1024)}, u32[]{:S(2)}) copy-start(f32[7168]{0:T(1024)} %param.17) | copy-start | bytes 86020
  62.3 12.8 %copy-start.8 = (f32[8,8,896]{2,1,0:T(8,128)}, f32[8,8,896]{2,1,0:T(8,128)S(1)}, u32[]{:S(2)}) copy-start(f32[8,8,896]{2,1,0:T(8,128)S(1)} %all-to-all-done) | copy-start | bytes 688132
  62.3 12.8 %all-to-all-start.4 = ((f32[8,8,896]{2,1,0:T(8,128)}), f32[8,8,896]{2,1,0:T(8,128)S(1)}, u32[]{:S(2)}, u32[]{:S(2)}) async-start(f32[8,8,896]{2,1,0:T(8,128)} %convolution_bitcast_fusion.2), calls=%async_computation.4 | async-start | bytes 458752 | tf_op jit(solution)/shard_map/all_to_all | solution.py:93
  67.1 52.5 %all-reduce.5.cloned.1.call-start = ((), (), s32[]{:S(2)}) async-start(), calls=%async_computation.7 | async-start | bytes 917504 | tf_op jit(solution)/shard_map/psum | solution.py:94
  75.1 0.7 copy-start.9
  123.1 28.6 %all-to-all-start.5 = ((bf16[8,8,7168]{2,1,0:T(8,128)(2,1)}), bf16[8,8,7168]{2,1,0:T(8,128)(2,1)S(1)}, u32[]{:S(2)}, u32[]{:S(2)}) async-start(bf16[8,8,7168]{2,1,0:T(8,128)(2,1)} %bitcast.41), calls=%async_computation.5 | async-start | bytes 1835008 | tf_op jit(solution)/shard_map/all_to_all | solution.py:101
  142.5 15.0 %copy-start.5 = (f32[8,7168]{1,0:T(8,128)S(1)}, f32[8,7168]{1,0:T(8,128)}, u32[]{:S(2)}) copy-start(f32[8,7168]{1,0:T(8,128)} %get-tuple-element.7) | copy-start | bytes 688132
  151.8 46.0 %all-to-all-start.2 = ((bf16[1,1792,2,512]{1,2,0,3:T(2,128)(2,1)}), bf16[1,1792,2,512]{1,2,0,3:T(2,128)(2,1)}, u32[]{:S(2)}, u32[]{:S(2)}) async-start(bf16[1,1792,2,512]{1,2,0,3:T(2,128)(2,1)} %copy.48), calls=%async_computation.2 | async-start | bytes 7340032 | tf_op jit(solution)/shard_map/all_to_all | solution.py:83
  199.8 28.6 %all-to-all-start.1 = ((bf16[8,8,7168]{2,1,0:T(8,128)(2,1)}), bf16[8,8,7168]{2,1,0:T(8,128)(2,1)}, u32[]{:S(2)}, u32[]{:S(2)}) async-start(bf16[8,8,7168]{2,1,0:T(8,128)(2,1)} %bitcast.14), calls=%async_computation.1 | async-start | bytes 1835008 | tf_op jit(solution)/shard_map/all_to_all | solution.py:101
  210.9 1.9 copy-start.1
  210.9 3.1 copy-start.2
  228.4 27.3 %all-to-all-start.6 = ((bf16[8,8,7168]{2,1,0:T(8,128)(2,1)}), bf16[8,8,7168]{2,1,0:T(8,128)(2,1)S(1)}, u32[]{:S(2)}, u32[]{:S(2)}) async-start(bf16[8,8,7168]{2,1,0:T(8,128)(2,1)} %convolution_convert_fusion), calls=%async_computation.6 | async-start | bytes 1835008 | tf_op jit(solution)/shard_map/all_to_all | solution.py:113
  232.7 3.7 %copy-start.3 = (bf16[1,128,7168]{2,1,0:T(8,128)(2,1)S(1)}, bf16[1,128,7168]{2,1,0:T(8,128)(2,1)}, u32[]{:S(2)}) copy-start(bf16[1,128,7168]{2,1,0:T(8,128)(2,1)} %param.21) | copy-start | bytes 5505028
  236.4 24.2 %copy-start.12 = (f32[2,8,4]{1,2,0:T(4,128)S(1)}, f32[2,8,4]{1,2,0:T(4,128)}, u32[]{:S(2)}) copy-start(f32[2,8,4]{1,2,0:T(4,128)} %param.16) | copy-start | bytes 772
  255.7 28.0 %all-to-all-start.3 = ((bf16[8,8,7168]{2,1,0:T(8,128)(2,1)}), bf16[8,8,7168]{2,1,0:T(8,128)(2,1)}, u32[]{:S(2)}, u32[]{:S(2)}) async-start(bf16[8,8,7168]{2,1,0:T(8,128)(2,1)} %convolution_convert_fusion.1), calls=%async_computation.3 | async-start | bytes 1835008 | tf_op jit(solution)/shard_map/all_to_all | solution.py:113
  260.7 67.6 %all-reduce.7.cloned.1.call-start = ((), (), s32[]{:S(2)}) async-start(), calls=%async_computation.8 | async-start | bytes 458752 | tf_op jit(solution)/shard_map/psum | solution.py:118
  261.5 66.8 %copy-start.6 = (f32[8,7168]{1,0:T(8,128)S(1)}, f32[8,7168]{1,0:T(8,128)}, u32[]{:S(2)}) copy-start(f32[8,7168]{1,0:T(8,128)} %get-tuple-element.8) | copy-start | bytes 688132
  329.3 0.7 copy-start.15
Sparse Core Ops, SparseCore 0:
  75.9 43.6 all-reduce.4
  287.7 40.5 all-reduce.6
where the time goes:
time: 339 us; the launch traced here: 337 us
  waiting for transfers between devices  191 us (56%)
  starting transfers between devices  34.9 us (10%)
  local copies, waits for them, and re-layouts  31.5 us (9%)
  matrix products  30.6 us (9%)
  blocking collectives  30.4 us (9%)
  between operations  13.6 us (4%)
  other arithmetic  4.89 us (1%)
    psum x1, waiting for transfers between devices, local(): attended = lax.psum(own_rows, 'group')  43.1 us
    psum x1, waiting for transfers between devices, local(): lax.psum(expert_mix.astype(jnp.bfloat16), 'group').astype(jnp.float32)  40.7 us
    all_to_all x1, waiting for transfers between devices, local(): lax.all_to_all(gate_up, 'group', split_axis=3, concat_axis=1, tiled=True)  39.2 us
    all_to_all x2, waiting for transfers between devices, local(): lax.all_to_all(block_part.astype(jnp.bfloat16), 'ep', split_axis=0, conca...  37.7 us
    all_gather x2, blocking collectives, local(): lax.all_gather(head_values, 'ep', axis=0, tiled=True)  30.4 us
    all_to_all x2, waiting for transfers between devices, local(): lax.all_to_all(outgoing, 'ep', split_axis=0, concat_axis=0, tiled=True)  22.3 us
    unnamed x34, local copies, waits for them, and re-layouts  17.5 us
    all_to_all x2, starting transfers between devices, local(): lax.all_to_all(outgoing, 'ep', split_axis=0, concat_axis=0, tiled=True)  11.3 us
  transfers between devices with their start and end apart: 9, of which 8 were waited for; matrix products, arithmetic and copies ran while one was open for 12% of the time, Pallas kernels for 0%

commit v1 on v0

--- a/solution.py
+++ b/solution.py
@@ -1,8 +1,11 @@
+import functools
 import math
 
 import jax
 import jax.numpy as jnp
 from jax import lax
+from jax.experimental import pallas as pl
+from jax.experimental.pallas import tpu as pltpu
 from jax.sharding import PartitionSpec as P
 
 ROPE = 64
@@ -120,9 +123,406 @@
     return jnp.stack(results)
 
 
+MESH = pl.DeviceIdType.MESH
+BF = jnp.bfloat16
+F32 = jnp.float32
+
+
+def layer_kernel(
+    ng,
+    nep,
+    hv_ref,
+    hid_ref,
+    coef_ref,
+    gain_ref,
+    wo_hbm,
+    gu_hbm,
+    dn_hbm,
+    out_ref,
+    wo,
+    gu,
+    dn,
+    heads,
+    hid_blk,
+    coefs,
+    s_own,
+    s_send,
+    s_rx,
+    ag,
+    ssq_own,
+    ssq_rx,
+    res,
+    pre_send,
+    pre_rx,
+    part,
+    sib_rx,
+    chip_sum,
+    grp_rx,
+    grp_sum,
+    z_rx,
+    fin,
+    load_sem,
+    send_sem,
+    heads_sem,
+    hid_sem,
+    coef_sem,
+    s_sem,
+    ag_sem,
+    ssq_sem,
+    res_sem,
+    pre_sem,
+    sib_sem,
+    grp_sem,
+    z_sem,
+    fin_sem,
+):
+    g = lax.axis_index("group")
+    j = lax.axis_index("ep")
+    nz = nep // 2
+    z = j // 2
+    c = j % 2
+    other = 1 - c
+    sibling = (g, z * 2 + other)
+    rows = hv_ref.shape[0]
+    block = wo.shape[1]
+    owners = nep // ng
+    band = owners * rows
+    slice_width = 2 * block
+
+    loads = [
+        pltpu.make_async_copy(wo_hbm, wo, load_sem.at[0]),
+        pltpu.make_async_copy(gu_hbm, gu, load_sem.at[1]),
+    ]
+    for s in range(ng):
+        loads.append(
+            pltpu.make_async_copy(
+                dn_hbm.at[:, pl.ds(s * slice_width, slice_width)], dn.at[s], load_sem.at[2 + s]
+            )
+        )
+    for load in loads:
+        load.start()
+
+    barrier = pltpu.get_barrier_semaphore()
+    ep_peers = [(g, (j + d) % nep) for d in range(1, nep)]
+    g_peers = [((g + d) % ng, j) for d in range(1, ng)]
+    for peer in ep_peers + g_peers:
+        pl.semaphore_signal(barrier, inc=1, device_id=peer, device_id_type=MESH)
+    pl.semaphore_wait(barrier, len(ep_peers) + len(g_peers))
+
+    sends = []
+
+    def remote(src, dst, recv, peer, index):
+        return pltpu.make_async_remote_copy(
+            src_ref=src,
+            dst_ref=dst,
+            send_sem=send_sem.at[index],
+            recv_sem=recv,
+            device_id=peer,
+            device_id_type=MESH,
+        )
+
+    def send(src, dst, recv, peer):
+        copy = remote(src, dst, recv, peer, len(sends))
+        copy.start()
+        sends.append(copy)
+
+    def arrived(dst, recv):
+        remote(dst, dst, recv, sibling, 0).wait_recv()
+
+    heads[j] = hv_ref[...]
+    for d in range(1, nz):
+        send(heads.at[j], heads.at[j], heads_sem.at[j], (g, (z + d) % nz * 2 + c))
+    send(heads.at[j], heads.at[j], heads_sem.at[j], sibling)
+    coefs[j] = coef_ref[...]
+    for peer in ep_peers:
+        send(coefs.at[j], coefs.at[j], coef_sem.at[j], peer)
+
+    hid_base = len(sends)
+    is_source = j // owners == g
+    hid_sends = []
+    for k, peer in enumerate(ep_peers):
+        start = pl.multiple_of(peer[1] * block, 128)
+        hid_sends.append(
+            remote(
+                hid_ref.at[:, pl.ds(start, block)],
+                hid_blk.at[j % owners],
+                hid_sem.at[j % owners],
+                peer,
+                send_sem.shape[0] - nep + k,
+            )
+        )
+
+    @pl.when(is_source)
+    def _():
+        for copy in hid_sends:
+            copy.start()
+        hid_blk[j % owners] = hid_ref[:, pl.ds(pl.multiple_of(j * block, 128), block)]
+
+    for d in range(1, nz):
+        slot = (z + d) % nz * 2 + c
+        arrived(heads.at[slot], heads_sem.at[slot])
+        send(heads.at[slot], heads.at[slot], heads_sem.at[slot], sibling)
+    for d in range(nz):
+        slot = (z + d) % nz * 2 + other
+        arrived(heads.at[slot], heads_sem.at[slot])
+
+    loads[0].wait()
+    spread = jnp.dot(
+        heads[...].reshape(nep * rows, heads.shape[2]), wo[...], preferred_element_type=F32
+    )
+    s_own[...] = spread.reshape(ng, band, block)
+    s_send[...] = spread.astype(BF).reshape(ng, band, block)
+    for peer in g_peers:
+        send(s_send.at[peer[0]], s_rx.at[g], s_sem.at[g], peer)
+    for i in range(owners):
+
+        @pl.when(g * owners + i != j)
+        def _(i=i):
+            arrived(hid_blk.at[i], hid_sem.at[i])
+
+    total = s_own[g] + hid_blk[...].reshape(band, block).astype(F32)
+    for d in range(1, ng):
+        slot = (g + d) % ng
+        arrived(s_rx.at[slot], s_sem.at[slot])
+        total = total + s_rx[slot].astype(F32)
+    ag[z] = total.astype(BF)
+
+    for d in range(1, nz):
+        send(ag.at[z], ag.at[z], ag_sem.at[z], (g, (z + d) % nz * 2 + c))
+    square = None
+    for d in range(nz):
+        slot = (z + d) % nz
+        if d:
+            arrived(ag.at[slot], ag_sem.at[slot])
+
+        @pl.when(slot != g)
+        def _(slot=slot, index=len(sends)):
+            remote(ag.at[slot], res.at[c, g], res_sem.at[c, g], (slot, j), index).start()
+
+        @pl.when(slot == g)
+        def _(slot=slot):
+            res[c, g] = ag[slot]
+
+        sends.append((slot, remote(ag.at[slot], res.at[c, g], res_sem.at[c, g], (slot, j), len(sends))))
+        value = ag[slot].astype(F32)
+        term = jnp.sum(value * value, axis=1, keepdims=True)
+        square = term if square is None else square + term
+    ssq_own[...] = jnp.broadcast_to(square, ssq_own.shape)
+    ssq_rx[c, g] = ssq_own[...]
+    for peer in g_peers:
+        send(ssq_own, ssq_rx.at[c, g], ssq_sem.at[c, g], peer)
+    for d in range(ng):
+        slot = (g + d) % ng
+        if d:
+            arrived(res.at[c, slot], res_sem.at[c, slot])
+        send(res.at[c, slot], res.at[c, slot], res_sem.at[c, slot], sibling)
+    for d in range(ng):
+        slot = (g + d) % ng
+        if d:
+            arrived(ssq_rx.at[c, slot], ssq_sem.at[c, slot])
+        send(ssq_rx.at[c, slot], ssq_rx.at[c, slot], ssq_sem.at[c, slot], sibling)
+    for d in range(ng):
+        slot = (g + d) % ng
+        arrived(res.at[other, slot], res_sem.at[other, slot])
+        arrived(ssq_rx.at[other, slot], ssq_sem.at[other, slot])
+
+    mean_square = (ssq_rx[0] + ssq_rx[1]).reshape(ng * band, 128)[:, :1] / (nep * block)
+    scale = lax.rsqrt(mean_square + 1e-06)
+    loads[1].wait()
+    pre = None
+    for b in range(2):
+        rows_in = res[b].reshape(ng * band, block).astype(F32)
+        normed = (rows_in * scale * gain_ref[2 * g + b]).astype(BF)
+        term = jnp.dot(normed, gu[pl.ds(b * block, block), :], preferred_element_type=F32)
+        pre = term if pre is None else pre + term
+    half = pre.shape[1] // 2
+    units = half // ng
+    for s in range(ng):
+        pre_send[s, :, :units] = pre[:, s * units : (s + 1) * units].astype(BF)
+        pre_send[s, :, units:] = pre[:, half + s * units : half + (s + 1) * units].astype(BF)
+    for peer in g_peers:
+        send(pre_send.at[peer[0]], pre_rx.at[g], pre_sem.at[g], peer)
+    pre_sum = pre_send[g].astype(F32)
+    for d in range(1, ng):
+        slot = (g + d) % ng
+        arrived(pre_rx.at[slot], pre_sem.at[slot])
+        pre_sum = pre_sum + pre_rx[slot].astype(F32)
+    activation = (jax.nn.silu(pre_sum[:, :units]) * pre_sum[:, units:]).astype(BF)
+    for peer in ep_peers:
+        arrived(coefs.at[peer[1]], coef_sem.at[peer[1]])
+    lane = lax.broadcasted_iota(jnp.int32, (nep * rows, 128), 1)
+    factor = jnp.sum(
+        jnp.where(lane == z, coefs[...].reshape(nep * rows, 128), 0.0), axis=1, keepdims=True
+    )
+    for load in loads[2:]:
+        load.wait()
+
+    order = [(g + d) % ng for d in list(range(1, ng)) + [0]]
+    for s in order:
+        piece = jnp.dot(activation, dn[s], preferred_element_type=F32) * factor
+        part[s] = piece.astype(BF).reshape(nz, 2, rows, slice_width)
+        send(part.at[s, :, other], sib_rx.at[s], sib_sem.at[s], sibling)
+    for s in order:
+        arrived(sib_rx.at[s], sib_sem.at[s])
+        chip_sum[s] = (part[s, :, c].astype(F32) + sib_rx[s].astype(F32)).astype(BF)
+        if s is not order[-1]:
+            send(chip_sum.at[s], grp_rx.at[g], grp_sem.at[g], (s, j))
+    summed = chip_sum[g].astype(F32)
+    for d in range(1, ng):
+        slot = (g + d) % ng
+        arrived(grp_rx.at[slot], grp_sem.at[slot])
+        summed = summed + grp_rx[slot].astype(F32)
+    grp_sum[...] = summed.astype(BF)
+    for d in range(1, nz):
+        pz = (z + d) % nz
+        send(grp_sum.at[pz], z_rx.at[z], z_sem.at[z], (g, pz * 2 + c))
+    own = grp_sum[z].astype(F32)
+    for d in range(1, nz):
+        slot = (z + d) % nz
+        arrived(z_rx.at[slot], z_sem.at[slot])
+        own = own + z_rx[slot].astype(F32)
+    first = pl.multiple_of(j % owners * rows, rows)
+    for b in range(2):
+        residual = res[b, j // owners, pl.ds(first, rows), :].astype(F32)
+        fin[g, :, b * block : (b + 1) * block] = (
+            residual + own[:, b * block : (b + 1) * block]
+        ).astype(BF)
+    for peer in g_peers:
+        send(fin.at[g], fin.at[g], fin_sem.at[g], peer)
+    for d in range(1, ng):
+        slot = (g + d) % ng
+        arrived(fin.at[slot], fin_sem.at[slot])
+    for s in range(ng):
+        out_ref[:, s * slice_width : (s + 1) * slice_width] = fin[s]
+
+    for copy in sends:
+        if isinstance(copy, tuple):
+
+            @pl.when(copy[0] != g)
+            def _(copy=copy):
+                copy[1].wait_send()
+
+        else:
+            copy.wait_send()
+
+    @pl.when(is_source)
+    def _():
+        for copy in hid_sends:
+            copy.wait_send()
+
+
+def fused_layer(head_values, hidden, coefficient, gain, out_proj, gate_up, down):
+    ng, nep = lax.axis_size("group"), lax.axis_size("ep")
+    nz, owners = nep // 2, nep // ng
+    rows, head_width = head_values.shape
+    block = out_proj.shape[1]
+    width, units = 2 * block, down.shape[0]
+    band = owners * rows
+    vmem, anywhere = pl.BlockSpec(memory_space=pltpu.VMEM), pl.BlockSpec(memory_space=pl.ANY)
+    dma = pltpu.SemaphoreType.DMA
+    return pl.pallas_call(
+        functools.partial(layer_kernel, ng, nep),
+        out_shape=jax.ShapeDtypeStruct((rows, nep * block), BF),
+        in_specs=[vmem] * 4 + [anywhere] * 3,
+        out_specs=vmem,
+        scratch_shapes=[
+            pltpu.VMEM(out_proj.shape, BF),
+            pltpu.VMEM(gate_up.shape, BF),
+            pltpu.VMEM((ng, units, width), BF),
+            pltpu.VMEM((nep, rows, head_width), BF),
+            pltpu.VMEM((owners, rows, block), BF),
+            pltpu.VMEM((nep, rows, 128), F32),
+            pltpu.VMEM((ng, band, block), F32),
+            pltpu.VMEM((ng, band, block), BF),
+            pltpu.VMEM((ng, band, block), BF),
+            pltpu.VMEM((nz, band, block), BF),
+            pltpu.VMEM((band, 128), F32),
+            pltpu.VMEM((2, ng, band, 128), F32),
+            pltpu.VMEM((2, ng, band, block), BF),
+            pltpu.VMEM((ng, nep * rows, 2 * units), BF),
+            pltpu.VMEM((ng, nep * rows, 2 * units), BF),
+            pltpu.VMEM((ng, nz, 2, rows, width), BF),
+            pltpu.VMEM((ng, nz, rows, width), BF),
+            pltpu.VMEM((ng, nz, rows, width), BF),
+            pltpu.VMEM((ng, nz, rows, width), BF),
+            pltpu.VMEM((nz, rows, width), BF),
+            pltpu.VMEM((nz, rows, width), BF),
+            pltpu.VMEM((ng, rows, width), BF),
+            dma((2 + ng,)),
+            dma((96,)),
+            dma((nep,)),
+            dma((owners,)),
+            dma((nep,)),
+            dma((ng,)),
+            dma((nz,)),
+            dma((2, ng)),
+            dma((2, ng)),
+            dma((ng,)),
+            dma((ng,)),
+            dma((ng,)),
+            dma((nz,)),
+            dma((ng,)),
+        ],
+        compiler_params=pltpu.CompilerParams(
+            collective_id=0, has_side_effects=True, vmem_limit_bytes=48 * 1024 * 1024
+        ),
+    )(head_values, hidden, coefficient, gain, out_proj, gate_up, down)
+
+
+def local_dense(
+    hidden_in,
+    queries,
+    latent_cache,
+    cache_lengths,
+    expert_ids,
+    gate_values,
+    norm_gain,
+    value_up,
+    out_proj,
+    gate_up,
+    down_proj,
+):
+    nep = lax.axis_size("ep")
+    micro, row_local, feature_count = hidden_in.shape
+    rows = micro * row_local
+
+    def merged(array):
+        return array.reshape((rows,) + array.shape[2:])
+
+    head_values = attend(
+        merged(queries), merged(latent_cache), cache_lengths.reshape(rows), value_up
+    )
+    named = merged(expert_ids)[:, :, None] == jnp.arange(128, dtype=jnp.int32)[None, None, :]
+    coefficient = jnp.sum(jnp.where(named, merged(gate_values)[:, :, None], 0.0), axis=1)
+    result = fused_layer(
+        head_values,
+        merged(hidden_in),
+        coefficient,
+        norm_gain.reshape(nep, 1, feature_count // nep),
+        out_proj,
+        gate_up[0].reshape(gate_up.shape[1], -1),
+        down_proj[0],
+    )
+    return result.reshape(hidden_in.shape)
+
+
+def layer(*args):
+    hidden_in, expert_ids, down_proj = args[0], args[4], args[10]
+    ng, nep = lax.axis_size("group"), lax.axis_size("ep")
+    micro, row_local, feature_count = hidden_in.shape
+    dense = (
+        2 * expert_ids.shape[2] == nep
+        and nep == 2 * ng
+        and feature_count % (nep * 128) == 0
+        and micro * row_local % 16 == 0
+        and down_proj.shape[1] % 128 == 0
+    )
+    return local_dense(*args) if dense else local(*args)
+
+
 def solution(mesh):
     return jax.shard_map(
-        local,
+        layer,
         mesh=mesh,
         in_specs=(
             P(None, "ep", None),

time: 339 us -> 79.3 us (0.23)
  waiting for transfers between devices: 191 us -> 0 us
  Pallas kernels: 0 us -> 63.3 us
  starting transfers between devices: 34.9 us -> 0 us
  blocking collectives: 30.4 us -> 0 us
  local copies, waits for them, and re-layouts: 31.5 us -> 7.05 us
  matrix products: 30.6 us -> 7.44 us
  between operations: 13.6 us -> 0.08 us
  other arithmetic: 4.89 us -> 0.16 us
    all_to_all x7 -> x0, waiting for transfers between devices: 107 us -> none  [the longest x1 39.2 us: local(): lax.all_to_all(gate_up, 'group', split_axis=3, concat_axis=1, tiled=True)]
    psum x2 -> x0, waiting for transfers between devices: 83.8 us -> none  [the longest x1 43.1 us: local(): attended = lax.psum(own_rows, 'group')]
    pallas_call x0 -> x1, Pallas kernels: none -> 63.3 us  [fused_layer(): pl.pallas_call(functools.partial(layer_kernel, ng, nep), out_shape=jax.Sh...]
    all_to_all x7 -> x0, starting transfers between devices: 34.9 us -> none  [the longest x2 11.3 us: local(): lax.all_to_all(outgoing, 'ep', split_axis=0, concat_axis=0, tiled=True)]
    all_gather x2 -> x0, blocking collectives: 30.4 us -> none  [local(): lax.all_gather(head_values, 'ep', axis=0, tiled=True)]
    dot_general x16 -> x0, matrix products: 25.2 us -> none  [the longest x2 6.88 us: local(): jnp.dot(lax.all_gather(head_values, 'ep', axis=0, tiled=True), out_proj,...]
    unnamed x34 -> x16, local copies, waits for them, and re-layouts: 17.5 us -> 5.97 us
    squeeze x4 -> x0, local copies, waits for them, and re-layouts: 5.43 us -> none  [the longest x1 5.26 us: local(): latent_cache[micro]]
  transfers between devices with their start and end apart: 9 -> 0, of which waited for: 8 -> 0; matrix products, arithmetic and copies ran while one was open for 12% -> 0% of each run, Pallas kernels for 0% -> 0%
where the time goes in v1:
time: 79.3 us; the launch traced here: 78 us
  Pallas kernels  63.3 us (80%)
  matrix products  7.44 us (9%)
  local copies, waits for them, and re-layouts  7.05 us (9%)
    pallas_call x1, Pallas kernels, fused_layer(): pl.pallas_call(functools.partial(layer_kernel, ng, nep), out_shape=jax.Sh...  63.3 us
    unnamed x16, local copies, waits for them, and re-layouts  5.97 us
    dot_general x1, matrix products, attend(): jnp.einsum('rhl,rlc->rhc', weights, cache[:, :, :latent_width], preferred...  3.53 us
    sub x1, matrix products, attend(): exponent = jnp.where(in_range, jnp.exp(masked - peak_score), 0.0)  3.39 us

profile of v1, /device:TPU:1, one launch (start us, length us, event | category | flops | bytes accessed | tf_op | source)
XLA Modules:
  0.0 78.0 jit_solution(8680671399394608017)
XLA Ops:
  0.0 0.0 copy-start
  0.0 0.9 %lt.21 = s32[16]{0:T(128)S(1)} reshape(s32[2,8]{1,0:T(2,128)} %param.14) | data formatting | bytes 128 | tf_op jit(solution)/shard_map/lt | solution.py:22
  0.9 0.1 iota_compare_fusion.1
  1.0 0.7 copy.18
  1.7 0.1 eq.15
  1.8 0.7 copy.19
  2.5 0.1 broadcast_in_dim.39
  2.5 0.1 select_reduce_fusion.coef_ref
  2.6 3.4 %fusion.9 = (f32[16,16]{1,0:T(8,128)S(1)}, f32[16,16,256]{2,1,0:T(8,128)S(1)}) fusion(pred[16,256]{1,0:T(8,128)(4,1)S(1)} %iota_compare_fusion.1, bf16[16,16,576]{2,1,0:T(8,128)(2,1)} %bitcast.31, bf16[16,256,576]{1,2,0:T(8,128)(2,1)} %bitcast.28), kind=kOutput, calls=%fused_computation.17 | convolution fusion | flops 75825408 | bytes 5280768 | tf_op jit(solution)/shard_map/sub | solution.py:25
  6.0 0.0 copy-start.5
  6.0 3.5 %fusion.1 = bf16[16,16,512]{2,1,0:T(8,128)(2,1)S(1)} fusion(bf16[16,256,576]{1,2,0:T(8,128)(2,1)} %bitcast.29, f32[16,16,256]{2,1,0:T(8,128)S(1)} %get-tuple-element.6, f32[16,16]{1,0:T(8,128)S(1)} %get-tuple-element.5), kind=kOutput, calls=%fused_computation.1 | convolution fusion | flops 67239936 | bytes 4719616 | tf_op jit(solution)/shard_map/rhl,rlc->rhc/dot_general | solution.py:27
  9.6 0.0 copy-done
  9.6 0.5 fusion.7
  10.1 0.0 copy-start.1
  10.1 0.0 copy-start.2
  10.1 0.0 copy-start.3
  10.1 0.0 copy-start.4
  10.1 0.0 copy-done.5
  10.1 2.9 %copy.22 = bf16[224,8,2,512]{3,1,2,0:T(8,128)(2,1)} copy(bf16[224,8,2,512]{3,2,1,0:T(2,128)(2,1)S(1)} %bitcast.30) | data formatting | bytes 7340032
  13.0 0.0 copy-done.1
  13.0 1.0 %copy-done.2 = bf16[1,128,7168]{2,1,0:T(8,128)(2,1)S(1)} copy-done((bf16[1,128,7168]{2,1,0:T(8,128)(2,1)S(1)}, bf16[1,128,7168]{2,1,0:T(8,128)(2,1)}, u32[]{:S(2)}) %copy-start.2) | copy-done | bytes 1835032
  14.0 0.0 copy-done.3
  14.0 0.0 copy-done.4
  14.0 63.3 %shard_map.109 = bf16[16,7168]{1,0:T(8,128)(2,1)S(1)} custom-call(bf16[16,2048]{1,0:T(8,128)(2,1)S(1)} %bitcast.24, bf16[16,7168]{1,0:T(8,128)(2,1)S(1)} %bitcast.25, f32[16,128]{1,0:T(8,128)S(1)} %select_reduce_fusion.coef_ref, f32[8,1,896]{2,1,0:T(1,128)S(1)} %bitcast.26, bf16[2048,896]{1,0:T(8,128)(2,1)S(1)} %copy-done.1, bf16[1792,1024]{1,0:T(8,128)(2,1)} %bitcast.27, ...), custom_call_target="tpu_custom_call" | custom-call | tf_op jit(solution)/shard_map/pallas_call | solution.py:423
  77.3 0.7 copy.28
  (1 shorter events, 0.0 us)
Async XLA Ops:
  0.0 9.6 %copy-start = (bf16[16,512,128]{2,1,0:T(8,128)(2,1)S(1)}, bf16[16,512,128]{2,1,0:T(8,128)(2,1)}, u32[]{:S(2)}) copy-start(bf16[16,512,128]{2,1,0:T(8,128)(2,1)} %param.18) | copy-start | bytes 6291460
  6.0 4.1 %copy-start.5 = (bf16[1,1792,2,512]{3,2,1,0:T(2,128)(2,1)S(1)}, bf16[1,1792,2,512]{3,2,1,0:T(2,128)(2,1)}, u32[]{:S(2)}) copy-start(bf16[1,1792,2,512]{3,2,1,0:T(2,128)(2,1)} %param.20) | copy-start | bytes 11010052
  10.1 3.0 %copy-start.1 = (bf16[2048,896]{1,0:T(8,128)(2,1)S(1)}, bf16[2048,896]{1,0:T(8,128)(2,1)}, u32[]{:S(2)}) copy-start(bf16[2048,896]{1,0:T(8,128)(2,1)} %wo_hbm.1) | copy-start | bytes 11010052
  10.1 3.9 %copy-start.2 = (bf16[1,128,7168]{2,1,0:T(8,128)(2,1)S(1)}, bf16[1,128,7168]{2,1,0:T(8,128)(2,1)}, u32[]{:S(2)}) copy-start(bf16[1,128,7168]{2,1,0:T(8,128)(2,1)} %param.21) | copy-start | bytes 5505028
  10.1 3.9 %copy-start.3 = (bf16[2,8,7168]{2,1,0:T(8,128)(2,1)S(1)}, bf16[2,8,7168]{2,1,0:T(8,128)(2,1)}, u32[]{:S(2)}) copy-start(bf16[2,8,7168]{2,1,0:T(8,128)(2,1)} %param.11) | copy-start | bytes 688132
  10.1 3.9 %copy-start.4 = (f32[7168]{0:T(1024)S(1)}, f32[7168]{0:T(1024)}, u32[]{:S(2)}) copy-start(f32[7168]{0:T(1024)} %param.17) | copy-start | bytes 86020

commit v2 on v1

--- a/solution.py
+++ b/solution.py
@@ -128,20 +128,53 @@
 F32 = jnp.float32
 
 
+def attend_rows(len_ref, q_ref, cache, cache_loads, latents):
+    rows, head_count = q_ref.shape[:2]
+    length = cache.shape[1]
+    latent_width = latents.shape[2]
+    chunk = rows // len(cache_loads)
+    score_scale = 1.0 / math.sqrt(NOPE + ROPE)
+    position = lax.broadcasted_iota(jnp.int32, (head_count, length), 1)
+    for r in range(rows):
+        if r % chunk == 0:
+            cache_loads[r // chunk].wait()
+        keys = cache[r]
+        scores = (
+            lax.dot_general(
+                q_ref[r], keys, (((1,), (1,)), ((), ())), preferred_element_type=F32
+            )
+            * score_scale
+        )
+        in_range = position < len_ref[r // len_ref.shape[1], r % len_ref.shape[1]]
+        masked = jnp.where(in_range, scores, -1e30)
+        peak_score = jnp.max(masked, axis=1, keepdims=True)
+        exponent = jnp.where(in_range, jnp.exp(masked - peak_score), 0.0)
+        weights = (exponent / jnp.sum(exponent, axis=1, keepdims=True)).astype(BF)
+        latents[r] = jnp.dot(
+            weights, keys[:, :latent_width], preferred_element_type=F32
+        ).astype(BF)
+
+
 def layer_kernel(
     ng,
     nep,
-    hv_ref,
+    len_ref,
+    q_ref,
     hid_ref,
     coef_ref,
     gain_ref,
+    cache_hbm,
+    vu_hbm,
     wo_hbm,
     gu_hbm,
     dn_hbm,
     out_ref,
+    cache,
+    vu,
     wo,
     gu,
     dn,
+    latents,
     heads,
     hid_blk,
     coefs,
@@ -154,11 +187,10 @@
     res,
     pre_send,
     pre_rx,
+    act,
     part,
     sib_rx,
     chip_sum,
-    grp_rx,
-    grp_sum,
     z_rx,
     fin,
     load_sem,
@@ -171,8 +203,9 @@
     ssq_sem,
     res_sem,
     pre_sem,
+    dn_sem,
+    act_sem,
     sib_sem,
-    grp_sem,
     z_sem,
     fin_sem,
 ):
@@ -183,23 +216,25 @@
     c = j % 2
     other = 1 - c
     sibling = (g, z * 2 + other)
-    rows = hv_ref.shape[0]
+    rows, head_count = q_ref.shape[:2]
     block = wo.shape[1]
     owners = nep // ng
     band = owners * rows
     slice_width = 2 * block
 
-    loads = [
-        pltpu.make_async_copy(wo_hbm, wo, load_sem.at[0]),
-        pltpu.make_async_copy(gu_hbm, gu, load_sem.at[1]),
+    chunk = rows // 4
+    cache_loads = [
+        pltpu.make_async_copy(
+            cache_hbm.at[pl.ds(i * chunk, chunk)], cache.at[pl.ds(i * chunk, chunk)], load_sem.at[i]
+        )
+        for i in range(4)
     ]
-    for s in range(ng):
-        loads.append(
-            pltpu.make_async_copy(
-                dn_hbm.at[:, pl.ds(s * slice_width, slice_width)], dn.at[s], load_sem.at[2 + s]
-            )
-        )
-    for load in loads:
+    vu_load = pltpu.make_async_copy(vu_hbm, vu, load_sem.at[4])
+    wo_load = pltpu.make_async_copy(wo_hbm, wo, load_sem.at[5])
+    gu_load = pltpu.make_async_copy(gu_hbm, gu, load_sem.at[6])
+    own_slice = pl.ds(pl.multiple_of(g * slice_width, 128), slice_width)
+    dn_load = pltpu.make_async_copy(dn_hbm.at[:, own_slice], dn.at[g], load_sem.at[7])
+    for load in cache_loads + [vu_load, wo_load, gu_load, dn_load]:
         load.start()
 
     barrier = pltpu.get_barrier_semaphore()
@@ -229,7 +264,25 @@
     def arrived(dst, recv):
         remote(dst, dst, recv, sibling, 0).wait_recv()
 
-    heads[j] = hv_ref[...]
+    for peer in g_peers:
+        start = pl.multiple_of(peer[0] * slice_width, 128)
+        send(dn_hbm.at[:, pl.ds(start, slice_width)], dn.at[g], dn_sem.at[g], peer)
+
+    attend_rows(len_ref, q_ref, cache, cache_loads, latents)
+    vu_load.wait()
+    count = rows * head_count
+    to = lax.broadcasted_iota(jnp.int32, (count, count), 0)
+    source = lax.broadcasted_iota(jnp.int32, (count, count), 1)
+    swap = jnp.where(source == to % rows * head_count + to // rows, 1.0, 0.0).astype(BF)
+    by_head = jnp.dot(
+        swap, latents[...].reshape(count, latents.shape[2]), preferred_element_type=F32
+    ).astype(BF)
+    value_width = vu.shape[2]
+    for h in range(head_count):
+        heads[j, :, h * value_width : (h + 1) * value_width] = jnp.dot(
+            by_head[h * rows : (h + 1) * rows], vu[h], preferred_element_type=F32
+        ).astype(BF)
+
     for d in range(1, nz):
         send(heads.at[j], heads.at[j], heads_sem.at[j], (g, (z + d) % nz * 2 + c))
     send(heads.at[j], heads.at[j], heads_sem.at[j], sibling)
@@ -266,7 +319,7 @@
         slot = (z + d) % nz * 2 + other
         arrived(heads.at[slot], heads_sem.at[slot])
 
-    loads[0].wait()
+    wo_load.wait()
     spread = jnp.dot(
         heads[...].reshape(nep * rows, heads.shape[2]), wo[...], preferred_element_type=F32
     )
@@ -328,7 +381,7 @@
 
     mean_square = (ssq_rx[0] + ssq_rx[1]).reshape(ng * band, 128)[:, :1] / (nep * block)
     scale = lax.rsqrt(mean_square + 1e-06)
-    loads[1].wait()
+    gu_load.wait()
     pre = None
     for b in range(2):
         rows_in = res[b].reshape(ng * band, block).astype(F32)
@@ -347,53 +400,54 @@
         slot = (g + d) % ng
         arrived(pre_rx.at[slot], pre_sem.at[slot])
         pre_sum = pre_sum + pre_rx[slot].astype(F32)
-    activation = (jax.nn.silu(pre_sum[:, :units]) * pre_sum[:, units:]).astype(BF)
+    act[g] = (jax.nn.silu(pre_sum[:, :units]) * pre_sum[:, units:]).astype(BF)
+    for peer in g_peers:
+        send(act.at[g], act.at[g], act_sem.at[g], peer)
     for peer in ep_peers:
         arrived(coefs.at[peer[1]], coef_sem.at[peer[1]])
     lane = lax.broadcasted_iota(jnp.int32, (nep * rows, 128), 1)
     factor = jnp.sum(
         jnp.where(lane == z, coefs[...].reshape(nep * rows, 128), 0.0), axis=1, keepdims=True
     )
-    for load in loads[2:]:
-        load.wait()
-
-    order = [(g + d) % ng for d in list(range(1, ng)) + [0]]
-    for s in order:
-        piece = jnp.dot(activation, dn[s], preferred_element_type=F32) * factor
-        part[s] = piece.astype(BF).reshape(nz, 2, rows, slice_width)
-        send(part.at[s, :, other], sib_rx.at[s], sib_sem.at[s], sibling)
-    for s in order:
-        arrived(sib_rx.at[s], sib_sem.at[s])
-        chip_sum[s] = (part[s, :, c].astype(F32) + sib_rx[s].astype(F32)).astype(BF)
-        if s is not order[-1]:
-            send(chip_sum.at[s], grp_rx.at[g], grp_sem.at[g], (s, j))
-    summed = chip_sum[g].astype(F32)
+    dn_load.wait()
     for d in range(1, ng):
         slot = (g + d) % ng
-        arrived(grp_rx.at[slot], grp_sem.at[slot])
-        summed = summed + grp_rx[slot].astype(F32)
-    grp_sum[...] = summed.astype(BF)
-    for d in range(1, nz):
-        pz = (z + d) % nz
-        send(grp_sum.at[pz], z_rx.at[z], z_sem.at[z], (g, pz * 2 + c))
-    own = grp_sum[z].astype(F32)
-    for d in range(1, nz):
-        slot = (z + d) % nz
-        arrived(z_rx.at[slot], z_sem.at[slot])
-        own = own + z_rx[slot].astype(F32)
+        arrived(dn.at[slot], dn_sem.at[slot])
+    for d in range(1, ng):
+        slot = (g + d) % ng
+        arrived(act.at[slot], act_sem.at[slot])
+    activation = jnp.concatenate([act[s] for s in range(ng)], axis=1)
+
+    for b in range(2):
+        columns = dn[:, :, b * block : (b + 1) * block].reshape(ng * units, block)
+        piece = jnp.dot(activation, columns, preferred_element_type=F32) * factor
+        part[b] = piece.astype(BF).reshape(nz, 2, rows, block)
+        send(part.at[b, :, other], sib_rx.at[b], sib_sem.at[b], sibling)
+    for b in range(2):
+        arrived(sib_rx.at[b], sib_sem.at[b])
+        chip_sum[b] = (part[b, :, c].astype(F32) + sib_rx[b].astype(F32)).astype(BF)
+        for d in range(1, nz):
+            pz = (z + d) % nz
+            send(chip_sum.at[b, pz], z_rx.at[b, z], z_sem.at[b, z], (g, pz * 2 + c))
     first = pl.multiple_of(j % owners * rows, rows)
     for b in range(2):
+        own = chip_sum[b, z].astype(F32)
+        for d in range(1, nz):
+            slot = (z + d) % nz
+            arrived(z_rx.at[b, slot], z_sem.at[b, slot])
+            own = own + z_rx[b, slot].astype(F32)
         residual = res[b, j // owners, pl.ds(first, rows), :].astype(F32)
-        fin[g, :, b * block : (b + 1) * block] = (
-            residual + own[:, b * block : (b + 1) * block]
-        ).astype(BF)
-    for peer in g_peers:
-        send(fin.at[g], fin.at[g], fin_sem.at[g], peer)
-    for d in range(1, ng):
-        slot = (g + d) % ng
-        arrived(fin.at[slot], fin_sem.at[slot])
+        fin[b, g] = (residual + own).astype(BF)
+        for peer in g_peers:
+            send(fin.at[b, g], fin.at[b, g], fin_sem.at[b, g], peer)
+    for b in range(2):
+        for d in range(1, ng):
+            slot = (g + d) % ng
+            arrived(fin.at[b, slot], fin_sem.at[b, slot])
     for s in range(ng):
-        out_ref[:, s * slice_width : (s + 1) * slice_width] = fin[s]
+        for b in range(2):
+            start = (2 * s + b) * block
+            out_ref[:, start : start + block] = fin[b, s]
 
     for copy in sends:
         if isinstance(copy, tuple):
@@ -411,10 +465,13 @@
             copy.wait_send()
 
 
-def fused_layer(head_values, hidden, coefficient, gain, out_proj, gate_up, down):
+def fused_layer(
+    lengths, queries, hidden, coefficient, gain, cache, value_up, out_proj, gate_up, down
+):
     ng, nep = lax.axis_size("group"), lax.axis_size("ep")
     nz, owners = nep // 2, nep // ng
-    rows, head_width = head_values.shape
+    rows, head_count = queries.shape[:2]
+    head_width = head_count * value_up.shape[2]
     block = out_proj.shape[1]
     width, units = 2 * block, down.shape[0]
     band = owners * rows
@@ -423,12 +480,15 @@
     return pl.pallas_call(
         functools.partial(layer_kernel, ng, nep),
         out_shape=jax.ShapeDtypeStruct((rows, nep * block), BF),
-        in_specs=[vmem] * 4 + [anywhere] * 3,
+        in_specs=[pl.BlockSpec(memory_space=pltpu.SMEM)] + [vmem] * 4 + [anywhere] * 5,
         out_specs=vmem,
         scratch_shapes=[
+            pltpu.VMEM(cache.shape, BF),
+            pltpu.VMEM(value_up.shape, BF),
             pltpu.VMEM(out_proj.shape, BF),
             pltpu.VMEM(gate_up.shape, BF),
             pltpu.VMEM((ng, units, width), BF),
+            pltpu.VMEM((rows, head_count, value_up.shape[1]), BF),
             pltpu.VMEM((nep, rows, head_width), BF),
             pltpu.VMEM((owners, rows, block), BF),
             pltpu.VMEM((nep, rows, 128), F32),
@@ -441,14 +501,13 @@
             pltpu.VMEM((2, ng, band, block), BF),
             pltpu.VMEM((ng, nep * rows, 2 * units), BF),
             pltpu.VMEM((ng, nep * rows, 2 * units), BF),
-            pltpu.VMEM((ng, nz, 2, rows, width), BF),
-            pltpu.VMEM((ng, nz, rows, width), BF),
-            pltpu.VMEM((ng, nz, rows, width), BF),
-            pltpu.VMEM((ng, nz, rows, width), BF),
-            pltpu.VMEM((nz, rows, width), BF),
-            pltpu.VMEM((nz, rows, width), BF),
-            pltpu.VMEM((ng, rows, width), BF),
-            dma((2 + ng,)),
+            pltpu.VMEM((ng, nep * rows, units), BF),
+            pltpu.VMEM((2, nz, 2, rows, block), BF),
+            pltpu.VMEM((2, nz, rows, block), BF),
+            pltpu.VMEM((2, nz, rows, block), BF),
+            pltpu.VMEM((2, nz, rows, block), BF),
+            pltpu.VMEM((2, ng, rows, block), BF),
+            dma((8,)),
             dma((96,)),
             dma((nep,)),
             dma((owners,)),
@@ -460,13 +519,14 @@
             dma((ng,)),
             dma((ng,)),
             dma((ng,)),
-            dma((nz,)),
-            dma((ng,)),
+            dma((2,)),
+            dma((2, nz)),
+            dma((2, ng)),
         ],
         compiler_params=pltpu.CompilerParams(
             collective_id=0, has_side_effects=True, vmem_limit_bytes=48 * 1024 * 1024
         ),
-    )(head_values, hidden, coefficient, gain, out_proj, gate_up, down)
+    )(lengths, queries, hidden, coefficient, gain, cache, value_up, out_proj, gate_up, down)
 
 
 def local_dense(
@@ -489,16 +549,16 @@
     def merged(array):
         return array.reshape((rows,) + array.shape[2:])
 
-    head_values = attend(
-        merged(queries), merged(latent_cache), cache_lengths.reshape(rows), value_up
-    )
     named = merged(expert_ids)[:, :, None] == jnp.arange(128, dtype=jnp.int32)[None, None, :]
     coefficient = jnp.sum(jnp.where(named, merged(gate_values)[:, :, None], 0.0), axis=1)
     result = fused_layer(
-        head_values,
+        cache_lengths,
+        merged(queries),
         merged(hidden_in),
         coefficient,
         norm_gain.reshape(nep, 1, feature_count // nep),
+        merged(latent_cache),
+        value_up,
         out_proj,
         gate_up[0].reshape(gate_up.shape[1], -1),
         down_proj[0],

time: 79.3 us -> 82.4 us (1.039)
  local copies, waits for them, and re-layouts: 7.05 us -> 16.5 us
  matrix products: 7.44 us -> 0 us
  Pallas kernels: 63.3 us -> 64.8 us
    unnamed x16 -> x17, local copies, waits for them, and re-layouts: 5.97 us -> 16.4 us
    dot_general x2 -> x0, matrix products: 4.05 us -> none  [the longest x1 3.53 us: attend(): jnp.einsum('rhl,rlc->rhc', weights, cache[:, :, :latent_width], preferred...]
    sub x1 -> x0, matrix products: 3.39 us -> none  [attend(): exponent = jnp.where(in_range, jnp.exp(masked - peak_score), 0.0)]
    pallas_call x1, Pallas kernels: 63.3 us -> 64.8 us  [fused_layer(): pl.pallas_call(functools.partial(layer_kernel, ng, nep), out_shape=jax.Sh...]
    lt x1 -> x0, local copies, waits for them, and re-layouts: 0.91 us -> none  [attend(): jnp.arange(cache.shape[1], dtype=jnp.int32)[None, None, :]]
where the time goes in v2:
time: 82.4 us; the launch traced here: 81.4 us
  Pallas kernels  64.8 us (79%)
  local copies, waits for them, and re-layouts  16.5 us (20%)
    pallas_call x1, Pallas kernels, fused_layer(): pl.pallas_call(functools.partial(layer_kernel, ng, nep), out_shape=jax.Sh...  64.8 us
    unnamed x17, local copies, waits for them, and re-layouts  16.4 us

profile of v2, /device:TPU:1, one launch (start us, length us, event | category | flops | bytes accessed | tf_op | source)
XLA Modules:
  0.0 81.4 jit_solution(15969279081450073628)
XLA Ops:
  0.0 0.7 copy.17
  0.7 0.1 eq.15
  0.8 0.7 copy.18
  1.5 0.1 broadcast_in_dim.15
  1.5 0.1 select_reduce_fusion.coef_ref
  1.6 4.9 %copy.20 = bf16[224,8,2,512]{3,1,2,0:T(8,128)(2,1)} copy(bf16[224,8,2,512]{3,2,1,0:T(2,128)(2,1)} %bitcast.20) | data formatting | bytes 7340032
  6.5 0.0 copy-start
  6.5 0.0 copy-start.2
  6.5 0.0 copy-start.3
  6.5 0.0 copy-start.4
  6.6 0.0 copy-start.5
  6.6 7.9 %copy.19 = bf16[2,8,256,576]{3,2,1,0:T(8,128)(2,1)} copy(bf16[2,8,256,576]{2,3,1,0:T(8,128)(2,1)} %param.13) | data formatting | bytes 9437184 | tf_op args[2]
  14.4 0.0 copy-done
  14.4 0.0 copy-done.2
  14.4 0.0 copy-done.3
  14.4 0.0 copy-done.4
  14.4 0.0 copy-done.5
  14.5 0.0 copy-start.1
  14.5 1.5 %copy-done.1 = bf16[1,128,7168]{2,1,0:T(8,128)(2,1)S(1)} copy-done((bf16[1,128,7168]{2,1,0:T(8,128)(2,1)S(1)}, bf16[1,128,7168]{2,1,0:T(8,128)(2,1)}, u32[]{:S(2)}) %copy-start.1) | copy-done | bytes 1835032
  16.0 64.8 %shard_map.109 = bf16[16,7168]{1,0:T(8,128)(2,1)S(1)} custom-call(s32[2,8]{1,0:T(2,128)S(1)} %copy-done.5, bf16[16,16,576]{2,1,0:T(8,128)(2,1)S(1)} %bitcast.15, bf16[16,7168]{1,0:T(8,128)(2,1)S(1)} %bitcast.16, f32[16,128]{1,0:T(8,128)S(1)} %select_reduce_fusion.coef_ref, f32[8,1,896]{2,1,0:T(1,128)S(1)} %bitcast.17, bf16[16,256,576]{2,1,0:T(8,128)(2,1)} %bitcast.18, ...), custom_call_target="tpu_custom_call" | custom-call | tf_op jit(solution)/shard_map/pallas_call | solution.py:480
  80.7 0.7 copy.22
Async XLA Ops:
  6.5 7.9 %copy-start = (bf16[16,512,128]{2,1,0:T(8,128)(2,1)S(1)}, bf16[16,512,128]{2,1,0:T(8,128)(2,1)}, u32[]{:S(2)}) copy-start(bf16[16,512,128]{2,1,0:T(8,128)(2,1)} %vu_hbm.1) | copy-start | bytes 6291460
  6.5 7.9 %copy-start.2 = (bf16[2,8,16,576]{3,2,1,0:T(8,128)(2,1)S(1)}, bf16[2,8,16,576]{3,2,1,0:T(8,128)(2,1)}, u32[]{:S(2)}) copy-start(bf16[2,8,16,576]{3,2,1,0:T(8,128)(2,1)} %param.12) | copy-start | bytes 884740
  6.5 7.9 %copy-start.3 = (bf16[2,8,7168]{2,1,0:T(8,128)(2,1)S(1)}, bf16[2,8,7168]{2,1,0:T(8,128)(2,1)}, u32[]{:S(2)}) copy-start(bf16[2,8,7168]{2,1,0:T(8,128)(2,1)} %param.11) | copy-start | bytes 688132
  6.5 7.9 %copy-start.4 = (f32[7168]{0:T(1024)S(1)}, f32[7168]{0:T(1024)}, u32[]{:S(2)}) copy-start(f32[7168]{0:T(1024)} %param.17) | copy-start | bytes 86020
  6.6 7.9 %copy-start.5 = (s32[2,8]{1,0:T(2,128)S(1)}, s32[2,8]{1,0:T(2,128)}, u32[]{:S(2)}) copy-start(s32[2,8]{1,0:T(2,128)} %len_ref.1) | copy-start | bytes 196
  14.5 1.5 %copy-start.1 = (bf16[1,128,7168]{2,1,0:T(8,128)(2,1)S(1)}, bf16[1,128,7168]{2,1,0:T(8,128)(2,1)}, u32[]{:S(2)}) copy-start(bf16[1,128,7168]{2,1,0:T(8,128)(2,1)} %param.21) | copy-start | bytes 5505028

commit v3 on v2

--- a/solution.py
+++ b/solution.py
@@ -128,31 +128,32 @@
 F32 = jnp.float32
 
 
-def attend_rows(len_ref, q_ref, cache, cache_loads, latents):
+def attend_rows(len_ref, q_ref, cache, cache_loads, latent_width):
     rows, head_count = q_ref.shape[:2]
-    length = cache.shape[1]
-    latent_width = latents.shape[2]
+    length = cache.shape[2]
     chunk = rows // len(cache_loads)
     score_scale = 1.0 / math.sqrt(NOPE + ROPE)
     position = lax.broadcasted_iota(jnp.int32, (head_count, length), 1)
+    masked = []
     for r in range(rows):
         if r % chunk == 0:
             cache_loads[r // chunk].wait()
-        keys = cache[r]
-        scores = (
-            lax.dot_general(
-                q_ref[r], keys, (((1,), (1,)), ((), ())), preferred_element_type=F32
-            )
-            * score_scale
-        )
+        scores = jnp.dot(q_ref[r], cache[r], preferred_element_type=F32) * score_scale
         in_range = position < len_ref[r // len_ref.shape[1], r % len_ref.shape[1]]
-        masked = jnp.where(in_range, scores, -1e30)
-        peak_score = jnp.max(masked, axis=1, keepdims=True)
-        exponent = jnp.where(in_range, jnp.exp(masked - peak_score), 0.0)
-        weights = (exponent / jnp.sum(exponent, axis=1, keepdims=True)).astype(BF)
-        latents[r] = jnp.dot(
-            weights, keys[:, :latent_width], preferred_element_type=F32
+        masked.append(jnp.where(in_range, scores, -1e30))
+    masked = jnp.concatenate(masked, axis=0)
+    exponent = jnp.exp(masked - jnp.max(masked, axis=1, keepdims=True))
+    weights = (exponent / jnp.sum(exponent, axis=1, keepdims=True)).astype(BF)
+    latents = [
+        lax.dot_general(
+            weights[r * head_count : (r + 1) * head_count],
+            cache[r, :latent_width, :],
+            (((1,), (1,)), ((), ())),
+            preferred_element_type=F32,
         ).astype(BF)
+        for r in range(rows)
+    ]
+    return jnp.concatenate(latents, axis=0)
 
 
 def layer_kernel(
@@ -161,7 +162,8 @@
     len_ref,
     q_ref,
     hid_ref,
-    coef_ref,
+    id_ref,
+    gate_ref,
     gain_ref,
     cache_hbm,
     vu_hbm,
@@ -174,7 +176,6 @@
     wo,
     gu,
     dn,
-    latents,
     heads,
     hid_blk,
     coefs,
@@ -222,19 +223,24 @@
     band = owners * rows
     slice_width = 2 * block
 
-    chunk = rows // 4
+    chunk = rows // 2
     cache_loads = [
         pltpu.make_async_copy(
             cache_hbm.at[pl.ds(i * chunk, chunk)], cache.at[pl.ds(i * chunk, chunk)], load_sem.at[i]
         )
-        for i in range(4)
+        for i in range(2)
     ]
     vu_load = pltpu.make_async_copy(vu_hbm, vu, load_sem.at[4])
     wo_load = pltpu.make_async_copy(wo_hbm, wo, load_sem.at[5])
-    gu_load = pltpu.make_async_copy(gu_hbm, gu, load_sem.at[6])
+    gu_loads = [
+        pltpu.make_async_copy(
+            gu_hbm.at[:, :, pl.ds(s * 128, 128)], gu.at[s], load_sem.at[8 + s]
+        )
+        for s in range(ng)
+    ]
     own_slice = pl.ds(pl.multiple_of(g * slice_width, 128), slice_width)
     dn_load = pltpu.make_async_copy(dn_hbm.at[:, own_slice], dn.at[g], load_sem.at[7])
-    for load in cache_loads + [vu_load, wo_load, gu_load, dn_load]:
+    for load in cache_loads + [vu_load, wo_load, dn_load] + gu_loads:
         load.start()
 
     barrier = pltpu.get_barrier_semaphore()
@@ -268,15 +274,13 @@
         start = pl.multiple_of(peer[0] * slice_width, 128)
         send(dn_hbm.at[:, pl.ds(start, slice_width)], dn.at[g], dn_sem.at[g], peer)
 
-    attend_rows(len_ref, q_ref, cache, cache_loads, latents)
+    latents = attend_rows(len_ref, q_ref, cache, cache_loads, vu.shape[1])
     vu_load.wait()
     count = rows * head_count
     to = lax.broadcasted_iota(jnp.int32, (count, count), 0)
     source = lax.broadcasted_iota(jnp.int32, (count, count), 1)
     swap = jnp.where(source == to % rows * head_count + to // rows, 1.0, 0.0).astype(BF)
-    by_head = jnp.dot(
-        swap, latents[...].reshape(count, latents.shape[2]), preferred_element_type=F32
-    ).astype(BF)
+    by_head = jnp.dot(swap, latents, preferred_element_type=F32).astype(BF)
     value_width = vu.shape[2]
     for h in range(head_count):
         heads[j, :, h * value_width : (h + 1) * value_width] = jnp.dot(
@@ -286,7 +290,14 @@
     for d in range(1, nz):
         send(heads.at[j], heads.at[j], heads_sem.at[j], (g, (z + d) % nz * 2 + c))
     send(heads.at[j], heads.at[j], heads_sem.at[j], sibling)
-    coefs[j] = coef_ref[...]
+    lane = lax.broadcasted_iota(jnp.int32, (1, 128), 1)
+    micro, top_count, row_local = id_ref.shape
+    for r in range(rows):
+        row = jnp.zeros((1, 128), F32)
+        for k in range(top_count):
+            m, i = r // row_local, r % row_local
+            row = row + jnp.where(lane == id_ref[m, k, i], gate_ref[m, k, i], 0.0)
+        coefs[j, r : r + 1, :] = row
     for peer in ep_peers:
         send(coefs.at[j], coefs.at[j], coef_sem.at[j], peer)
 
@@ -381,18 +392,42 @@
 
     mean_square = (ssq_rx[0] + ssq_rx[1]).reshape(ng * band, 128)[:, :1] / (nep * block)
     scale = lax.rsqrt(mean_square + 1e-06)
-    gu_load.wait()
-    pre = None
+    pieces = []
     for b in range(2):
         rows_in = res[b].reshape(ng * band, block).astype(F32)
         normed = (rows_in * scale * gain_ref[2 * g + b]).astype(BF)
-        term = jnp.dot(normed, gu[pl.ds(b * block, block), :], preferred_element_type=F32)
-        pre = term if pre is None else pre + term
-    half = pre.shape[1] // 2
-    units = half // ng
-    for s in range(ng):
-        pre_send[s, :, :units] = pre[:, s * units : (s + 1) * units].astype(BF)
-        pre_send[s, :, units:] = pre[:, half + s * units : half + (s + 1) * units].astype(BF)
+        pieces += [normed[:, i : i + 128] for i in range(0, block, 128)]
+    feature = lax.broadcasted_iota(jnp.int32, (128, 512), 0)
+    place = lax.broadcasted_iota(jnp.int32, (128, 512), 1)
+    wanted = jnp.where(place < 256, 2 * feature, 256 + 2 * feature + 1)
+    spacing = jnp.where(place == wanted, 1.0, 0.0).astype(BF)
+    spaced = jnp.dot(
+        jnp.concatenate(pieces, axis=0), spacing, preferred_element_type=F32
+    ).astype(BF)
+    count = ng * band
+    features = jnp.concatenate(
+        [
+            jnp.concatenate(
+                [
+                    spaced[i * count : (i + 1) * count, :256],
+                    spaced[i * count : (i + 1) * count, 256:],
+                ],
+                axis=0,
+            )
+            for i in range(len(pieces))
+        ],
+        axis=1,
+    )
+    for load in gu_loads:
+        load.wait()
+    mixed = gu.reshape(ng, 2 * gu.shape[1], 128)
+    units = dn.shape[1]
+    for s in range(0, ng, 2):
+        columns = jnp.concatenate([mixed[s], mixed[s + 1]], axis=1)
+        pre = jnp.dot(features, columns, preferred_element_type=F32).astype(BF)
+        for i in range(2):
+            pre_send[s + i, :, :units] = pre[:count, i * 128 : (i + 1) * 128]
+            pre_send[s + i, :, units:] = pre[count:, i * 128 : (i + 1) * 128]
     for peer in g_peers:
         send(pre_send.at[peer[0]], pre_rx.at[g], pre_sem.at[g], peer)
     pre_sum = pre_send[g].astype(F32)
@@ -466,7 +501,7 @@
 
 
 def fused_layer(
-    lengths, queries, hidden, coefficient, gain, cache, value_up, out_proj, gate_up, down
+    lengths, queries, hidden, ids, gates, gain, cache, value_up, out_proj, gate_up, down
 ):
     ng, nep = lax.axis_size("group"), lax.axis_size("ep")
     nz, owners = nep // 2, nep // ng
@@ -476,19 +511,18 @@
     width, units = 2 * block, down.shape[0]
     band = owners * rows
     vmem, anywhere = pl.BlockSpec(memory_space=pltpu.VMEM), pl.BlockSpec(memory_space=pl.ANY)
-    dma = pltpu.SemaphoreType.DMA
+    smem, dma = pl.BlockSpec(memory_space=pltpu.SMEM), pltpu.SemaphoreType.DMA
     return pl.pallas_call(
         functools.partial(layer_kernel, ng, nep),
         out_shape=jax.ShapeDtypeStruct((rows, nep * block), BF),
-        in_specs=[pl.BlockSpec(memory_space=pltpu.SMEM)] + [vmem] * 4 + [anywhere] * 5,
+        in_specs=[smem, vmem, vmem, smem, smem, vmem] + [anywhere] * 5,
         out_specs=vmem,
         scratch_shapes=[
             pltpu.VMEM(cache.shape, BF),
             pltpu.VMEM(value_up.shape, BF),
             pltpu.VMEM(out_proj.shape, BF),
-            pltpu.VMEM(gate_up.shape, BF),
+            pltpu.VMEM((ng, gate_up.shape[0], 2, 128), BF),
             pltpu.VMEM((ng, units, width), BF),
-            pltpu.VMEM((rows, head_count, value_up.shape[1]), BF),
             pltpu.VMEM((nep, rows, head_width), BF),
             pltpu.VMEM((owners, rows, block), BF),
             pltpu.VMEM((nep, rows, 128), F32),
@@ -507,7 +541,7 @@
             pltpu.VMEM((2, nz, rows, block), BF),
             pltpu.VMEM((2, nz, rows, block), BF),
             pltpu.VMEM((2, ng, rows, block), BF),
-            dma((8,)),
+            dma((8 + ng,)),
             dma((96,)),
             dma((nep,)),
             dma((owners,)),
@@ -524,9 +558,9 @@
             dma((2, ng)),
         ],
         compiler_params=pltpu.CompilerParams(
-            collective_id=0, has_side_effects=True, vmem_limit_bytes=48 * 1024 * 1024
+            collective_id=0, has_side_effects=True, vmem_limit_bytes=60 * 1024 * 1024
         ),
-    )(lengths, queries, hidden, coefficient, gain, cache, value_up, out_proj, gate_up, down)
+    )(lengths, queries, hidden, ids, gates, gain, cache, value_up, out_proj, gate_up, down)
 
 
 def local_dense(
@@ -549,18 +583,17 @@
     def merged(array):
         return array.reshape((rows,) + array.shape[2:])
 
-    named = merged(expert_ids)[:, :, None] == jnp.arange(128, dtype=jnp.int32)[None, None, :]
-    coefficient = jnp.sum(jnp.where(named, merged(gate_values)[:, :, None], 0.0), axis=1)
     result = fused_layer(
         cache_lengths,
         merged(queries),
         merged(hidden_in),
-        coefficient,
+        jnp.swapaxes(expert_ids, 1, 2),
+        jnp.swapaxes(gate_values, 1, 2),
         norm_gain.reshape(nep, 1, feature_count // nep),
-        merged(latent_cache),
+        jnp.swapaxes(merged(latent_cache), 1, 2),
         value_up,
         out_proj,
-        gate_up[0].reshape(gate_up.shape[1], -1),
+        gate_up[0],
         down_proj[0],
     )
     return result.reshape(hidden_in.shape)
@@ -575,7 +608,8 @@
         and nep == 2 * ng
         and feature_count % (nep * 128) == 0
         and micro * row_local % 16 == 0
-        and down_proj.shape[1] % 128 == 0
+        and down_proj.shape[1] == 128
+        and ng % 2 == 0
     )
     return local_dense(*args) if dense else local(*args)
 

time: 82.4 us -> 68.1 us (0.83)
  local copies, waits for them, and re-layouts: 16.5 us -> 1.64 us
    unnamed x17 -> x1, local copies, waits for them, and re-layouts: 16.4 us -> 1.64 us
where the time goes in v3:
time: 68.1 us; the launch traced here: 67.1 us
  Pallas kernels  65.5 us (96%)
  local copies, waits for them, and re-layouts  1.64 us (2%)
    pallas_call x1, Pallas kernels, fused_layer(): pl.pallas_call(functools.partial(layer_kernel, ng, nep), out_shape=jax.Sh...  65.5 us
    unnamed x1, local copies, waits for them, and re-layouts  1.64 us

profile of v3, /device:TPU:1, one launch (start us, length us, event | category | flops | bytes accessed | tf_op | source)
XLA Modules:
  0.0 67.1 jit_solution(4318977768910955616)
XLA Ops:
  0.0 65.5 %shard_map.109 = bf16[16,7168]{1,0:T(8,128)(2,1)} custom-call(s32[2,8]{1,0:T(2,128)} %len_ref.1, bf16[16,16,576]{2,1,0:T(8,128)(2,1)} %bitcast.15, bf16[16,7168]{1,0:T(8,128)(2,1)} %bitcast.16, s32[2,4,8]{2,1,0:T(4,128)} %bitcast.18, f32[2,4,8]{2,1,0:T(4,128)} %bitcast.19, f32[8,1,896]{2,1,0:T(1,128)} %bitcast.17, bf16[16,576,256]{2,1,0:T(8,128)(2,1)} %bitcast.11, ...), custom_call_target="tpu_custom_call" | custom-call | tf_op jit(solution)/shard_map/pallas_call | solution.py:515
  65.5 1.6 %copy.13 = bf16[2,8,7168]{2,1,0:T(8,128)(2,1)} copy(bf16[2,8,7168]{2,1,0:T(8,128)(2,1)} %bitcast.14) | data formatting | bytes 458752

commit v4 on v3

--- a/solution.py
+++ b/solution.py
@@ -220,7 +220,7 @@
     rows, head_count = q_ref.shape[:2]
     block = wo.shape[1]
     owners = nep // ng
-    band = owners * rows
+    units = dn.shape[1]
     slice_width = 2 * block
 
     chunk = rows // 2
@@ -266,6 +266,15 @@
         copy = remote(src, dst, recv, peer, len(sends))
         copy.start()
         sends.append(copy)
+
+    def send_if(wanted, src, dst, recv, peer):
+        copy = remote(src, dst, recv, peer, len(sends))
+
+        @pl.when(wanted)
+        def _():
+            copy.start()
+
+        sends.append((wanted, copy))
 
     def arrived(dst, recv):
         remote(dst, dst, recv, sibling, 0).wait_recv()
@@ -301,7 +310,6 @@
     for peer in ep_peers:
         send(coefs.at[j], coefs.at[j], coef_sem.at[j], peer)
 
-    hid_base = len(sends)
     is_source = j // owners == g
     hid_sends = []
     for k, peer in enumerate(ep_peers):
@@ -326,153 +334,182 @@
         slot = (z + d) % nz * 2 + c
         arrived(heads.at[slot], heads_sem.at[slot])
         send(heads.at[slot], heads.at[slot], heads_sem.at[slot], sibling)
-    for d in range(nz):
-        slot = (z + d) % nz * 2 + other
-        arrived(heads.at[slot], heads_sem.at[slot])
+    count = nz * rows
+
+    def project(h):
+        @pl.when(other == h)
+        def _():
+            for d in range(nz):
+                slot = (z + d) % nz * 2 + other
+                arrived(heads.at[slot], heads_sem.at[slot])
+
+        rows_in = jnp.concatenate([heads[2 * i + h] for i in range(nz)], axis=0)
+        spread = jnp.dot(rows_in, wo[...], preferred_element_type=F32)
+        s_own[h] = spread.reshape(ng, rows, block)
+        s_send[h] = spread.astype(BF).reshape(ng, rows, block)
+        for peer in g_peers:
+            send(s_send.at[h, peer[0]], s_rx.at[h, g], s_sem.at[h, g], peer)
+
+    def add_heads(h):
+        @pl.when(g * 2 + h != j)
+        def _():
+            arrived(hid_blk.at[h], hid_sem.at[h])
+
+        total = s_own[h, g] + hid_blk[h].astype(F32)
+        for d in range(1, ng):
+            slot = (g + d) % ng
+            arrived(s_rx.at[h, slot], s_sem.at[h, slot])
+            total = total + s_rx[h, slot].astype(F32)
+        ag[h, z] = total.astype(BF)
+        for d in range(1, nz):
+            send(ag.at[h, z], ag.at[h, z], ag_sem.at[h, z], (g, (z + d) % nz * 2 + c))
+
+    def spread_blocks(h):
+        square = None
+        for d in range(nz):
+            slot = (z + d) % nz
+            if d:
+                arrived(ag.at[h, slot], ag_sem.at[h, slot])
+            send_if(
+                slot != g, ag.at[h, slot], res.at[h, c, g], res_sem.at[h, c, g], (slot, j)
+            )
+
+            @pl.when(slot == g)
+            def _(slot=slot):
+                res[h, c, g] = ag[h, slot]
+
+            value = ag[h, slot].astype(F32)
+            term = jnp.sum(value * value, axis=1, keepdims=True)
+            square = term if square is None else square + term
+        ssq_own[h] = jnp.broadcast_to(square, ssq_own.shape[1:])
+        ssq_rx[h, c, g] = ssq_own[h]
+        for peer in g_peers:
+            send(ssq_own.at[h], ssq_rx.at[h, c, g], ssq_sem.at[h, c, g], peer)
+
+    def share_blocks(h):
+        for ref, sem in ((res, res_sem), (ssq_rx, ssq_sem)):
+            for d in range(ng):
+                slot = (g + d) % ng
+                if d:
+                    arrived(ref.at[h, c, slot], sem.at[h, c, slot])
+                send(ref.at[h, c, slot], ref.at[h, c, slot], sem.at[h, c, slot], sibling)
+
+    def pre_activate(h):
+        for ref, sem in ((res, res_sem), (ssq_rx, ssq_sem)):
+            for d in range(ng):
+                slot = (g + d) % ng
+                arrived(ref.at[h, other, slot], sem.at[h, other, slot])
+        mean_square = (ssq_rx[h, 0] + ssq_rx[h, 1]).reshape(count, 128)[:, :1] / (nep * block)
+        scale = lax.rsqrt(mean_square + 1e-06)
+        pieces = []
+        for b in range(2):
+            rows_in = res[h, b].reshape(count, block).astype(F32)
+            normed = (rows_in * scale * gain_ref[2 * g + b]).astype(BF)
+            pieces += [normed[:, i : i + 128] for i in range(0, block, 128)]
+        feature = lax.broadcasted_iota(jnp.int32, (128, 512), 0)
+        place = lax.broadcasted_iota(jnp.int32, (128, 512), 1)
+        wanted = jnp.where(place < 256, 2 * feature, 256 + 2 * feature + 1)
+        spacing = jnp.where(place == wanted, 1.0, 0.0).astype(BF)
+        spaced = jnp.dot(
+            jnp.concatenate(pieces, axis=0), spacing, preferred_element_type=F32
+        ).astype(BF)
+        features = jnp.concatenate(
+            [
+                jnp.concatenate(
+                    [
+                        spaced[i * count : (i + 1) * count, :256],
+                        spaced[i * count : (i + 1) * count, 256:],
+                    ],
+                    axis=0,
+                )
+                for i in range(len(pieces))
+            ],
+            axis=1,
+        )
+        mixed = gu.reshape(ng, 2 * gu.shape[1], 128)
+        for s in range(0, ng, 2):
+            columns = jnp.concatenate([mixed[s], mixed[s + 1]], axis=1)
+            pre = jnp.dot(features, columns, preferred_element_type=F32).astype(BF)
+            for i in range(2):
+                pre_send[h, s + i, :, :units] = pre[:count, i * 128 : (i + 1) * 128]
+                pre_send[h, s + i, :, units:] = pre[count:, i * 128 : (i + 1) * 128]
+        for peer in g_peers:
+            send(pre_send.at[h, peer[0]], pre_rx.at[h, g], pre_sem.at[h, g], peer)
+
+    def activate(h):
+        pre_sum = pre_send[h, g].astype(F32)
+        for d in range(1, ng):
+            slot = (g + d) % ng
+            arrived(pre_rx.at[h, slot], pre_sem.at[h, slot])
+            pre_sum = pre_sum + pre_rx[h, slot].astype(F32)
+        act[h, g] = (jax.nn.silu(pre_sum[:, :units]) * pre_sum[:, units:]).astype(BF)
+        for peer in g_peers:
+            send(act.at[h, g], act.at[h, g], act_sem.at[h, g], peer)
+
+    def project_down(h):
+        for d in range(1, ng):
+            slot = (g + d) % ng
+            arrived(act.at[h, slot], act_sem.at[h, slot])
+        activation = jnp.concatenate([act[h, s] for s in range(ng)], axis=1)
+        lane = lax.broadcasted_iota(jnp.int32, (count, 128), 1)
+        gates = jnp.concatenate([coefs[2 * i + h] for i in range(nz)], axis=0)
+        factor = jnp.sum(jnp.where(lane == z, gates, 0.0), axis=1, keepdims=True)
+        for b in range(2):
+            columns = dn[:, :, b * block : (b + 1) * block].reshape(ng * units, block)
+            piece = jnp.dot(activation, columns, preferred_element_type=F32) * factor
+            part[h, b] = piece.astype(BF).reshape(nz, rows, block)
+            send_if(c != h, part.at[h, b], sib_rx.at[b], sib_sem.at[b], sibling)
+
+    def add_cores(h):
+        @pl.when(c == h)
+        def _():
+            for b in range(2):
+                arrived(sib_rx.at[b], sib_sem.at[b])
+                chip_sum[b] = (part[h, b].astype(F32) + sib_rx[b].astype(F32)).astype(BF)
+                for copy in z_sends[b]:
+                    copy.start()
 
     wo_load.wait()
-    spread = jnp.dot(
-        heads[...].reshape(nep * rows, heads.shape[2]), wo[...], preferred_element_type=F32
-    )
-    s_own[...] = spread.reshape(ng, band, block)
-    s_send[...] = spread.astype(BF).reshape(ng, band, block)
-    for peer in g_peers:
-        send(s_send.at[peer[0]], s_rx.at[g], s_sem.at[g], peer)
-    for i in range(owners):
-
-        @pl.when(g * owners + i != j)
-        def _(i=i):
-            arrived(hid_blk.at[i], hid_sem.at[i])
-
-    total = s_own[g] + hid_blk[...].reshape(band, block).astype(F32)
-    for d in range(1, ng):
-        slot = (g + d) % ng
-        arrived(s_rx.at[slot], s_sem.at[slot])
-        total = total + s_rx[slot].astype(F32)
-    ag[z] = total.astype(BF)
-
-    for d in range(1, nz):
-        send(ag.at[z], ag.at[z], ag_sem.at[z], (g, (z + d) % nz * 2 + c))
-    square = None
-    for d in range(nz):
-        slot = (z + d) % nz
-        if d:
-            arrived(ag.at[slot], ag_sem.at[slot])
-
-        @pl.when(slot != g)
-        def _(slot=slot, index=len(sends)):
-            remote(ag.at[slot], res.at[c, g], res_sem.at[c, g], (slot, j), index).start()
-
-        @pl.when(slot == g)
-        def _(slot=slot):
-            res[c, g] = ag[slot]
-
-        sends.append((slot, remote(ag.at[slot], res.at[c, g], res_sem.at[c, g], (slot, j), len(sends))))
-        value = ag[slot].astype(F32)
-        term = jnp.sum(value * value, axis=1, keepdims=True)
-        square = term if square is None else square + term
-    ssq_own[...] = jnp.broadcast_to(square, ssq_own.shape)
-    ssq_rx[c, g] = ssq_own[...]
-    for peer in g_peers:
-        send(ssq_own, ssq_rx.at[c, g], ssq_sem.at[c, g], peer)
-    for d in range(ng):
-        slot = (g + d) % ng
-        if d:
-            arrived(res.at[c, slot], res_sem.at[c, slot])
-        send(res.at[c, slot], res.at[c, slot], res_sem.at[c, slot], sibling)
-    for d in range(ng):
-        slot = (g + d) % ng
-        if d:
-            arrived(ssq_rx.at[c, slot], ssq_sem.at[c, slot])
-        send(ssq_rx.at[c, slot], ssq_rx.at[c, slot], ssq_sem.at[c, slot], sibling)
-    for d in range(ng):
-        slot = (g + d) % ng
-        arrived(res.at[other, slot], res_sem.at[other, slot])
-        arrived(ssq_rx.at[other, slot], ssq_sem.at[other, slot])
-
-    mean_square = (ssq_rx[0] + ssq_rx[1]).reshape(ng * band, 128)[:, :1] / (nep * block)
-    scale = lax.rsqrt(mean_square + 1e-06)
-    pieces = []
-    for b in range(2):
-        rows_in = res[b].reshape(ng * band, block).astype(F32)
-        normed = (rows_in * scale * gain_ref[2 * g + b]).astype(BF)
-        pieces += [normed[:, i : i + 128] for i in range(0, block, 128)]
-    feature = lax.broadcasted_iota(jnp.int32, (128, 512), 0)
-    place = lax.broadcasted_iota(jnp.int32, (128, 512), 1)
-    wanted = jnp.where(place < 256, 2 * feature, 256 + 2 * feature + 1)
-    spacing = jnp.where(place == wanted, 1.0, 0.0).astype(BF)
-    spaced = jnp.dot(
-        jnp.concatenate(pieces, axis=0), spacing, preferred_element_type=F32
-    ).astype(BF)
-    count = ng * band
-    features = jnp.concatenate(
-        [
-            jnp.concatenate(
-                [
-                    spaced[i * count : (i + 1) * count, :256],
-                    spaced[i * count : (i + 1) * count, 256:],
-                ],
-                axis=0,
-            )
-            for i in range(len(pieces))
-        ],
-        axis=1,
-    )
+    for h in range(2):
+        project(h)
+    for h in range(2):
+        add_heads(h)
+    for h in range(2):
+        spread_blocks(h)
+    for h in range(2):
+        share_blocks(h)
     for load in gu_loads:
         load.wait()
-    mixed = gu.reshape(ng, 2 * gu.shape[1], 128)
-    units = dn.shape[1]
-    for s in range(0, ng, 2):
-        columns = jnp.concatenate([mixed[s], mixed[s + 1]], axis=1)
-        pre = jnp.dot(features, columns, preferred_element_type=F32).astype(BF)
-        for i in range(2):
-            pre_send[s + i, :, :units] = pre[:count, i * 128 : (i + 1) * 128]
-            pre_send[s + i, :, units:] = pre[count:, i * 128 : (i + 1) * 128]
-    for peer in g_peers:
-        send(pre_send.at[peer[0]], pre_rx.at[g], pre_sem.at[g], peer)
-    pre_sum = pre_send[g].astype(F32)
-    for d in range(1, ng):
-        slot = (g + d) % ng
-        arrived(pre_rx.at[slot], pre_sem.at[slot])
-        pre_sum = pre_sum + pre_rx[slot].astype(F32)
-    act[g] = (jax.nn.silu(pre_sum[:, :units]) * pre_sum[:, units:]).astype(BF)
-    for peer in g_peers:
-        send(act.at[g], act.at[g], act_sem.at[g], peer)
+    for h in range(2):
+        pre_activate(h)
+    for h in range(2):
+        activate(h)
     for peer in ep_peers:
         arrived(coefs.at[peer[1]], coef_sem.at[peer[1]])
-    lane = lax.broadcasted_iota(jnp.int32, (nep * rows, 128), 1)
-    factor = jnp.sum(
-        jnp.where(lane == z, coefs[...].reshape(nep * rows, 128), 0.0), axis=1, keepdims=True
-    )
     dn_load.wait()
     for d in range(1, ng):
         slot = (g + d) % ng
         arrived(dn.at[slot], dn_sem.at[slot])
-    for d in range(1, ng):
-        slot = (g + d) % ng
-        arrived(act.at[slot], act_sem.at[slot])
-    activation = jnp.concatenate([act[s] for s in range(ng)], axis=1)
-
+    z_sends = []
     for b in range(2):
-        columns = dn[:, :, b * block : (b + 1) * block].reshape(ng * units, block)
-        piece = jnp.dot(activation, columns, preferred_element_type=F32) * factor
-        part[b] = piece.astype(BF).reshape(nz, 2, rows, block)
-        send(part.at[b, :, other], sib_rx.at[b], sib_sem.at[b], sibling)
-    for b in range(2):
-        arrived(sib_rx.at[b], sib_sem.at[b])
-        chip_sum[b] = (part[b, :, c].astype(F32) + sib_rx[b].astype(F32)).astype(BF)
+        z_sends.append([])
         for d in range(1, nz):
             pz = (z + d) % nz
-            send(chip_sum.at[b, pz], z_rx.at[b, z], z_sem.at[b, z], (g, pz * 2 + c))
-    first = pl.multiple_of(j % owners * rows, rows)
+            copy = remote(
+                chip_sum.at[b, pz], z_rx.at[b, z], z_sem.at[b, z], (g, pz * 2 + c), len(sends)
+            )
+            z_sends[b].append(copy)
+            sends.append(copy)
+    for h in range(2):
+        project_down(h)
+        add_cores(h)
     for b in range(2):
         own = chip_sum[b, z].astype(F32)
         for d in range(1, nz):
             slot = (z + d) % nz
             arrived(z_rx.at[b, slot], z_sem.at[b, slot])
             own = own + z_rx[b, slot].astype(F32)
-        residual = res[b, j // owners, pl.ds(first, rows), :].astype(F32)
-        fin[b, g] = (residual + own).astype(BF)
+        fin[b, g] = (res[c, b, z].astype(F32) + own).astype(BF)
         for peer in g_peers:
             send(fin.at[b, g], fin.at[b, g], fin_sem.at[b, g], peer)
     for b in range(2):
@@ -487,7 +524,7 @@
     for copy in sends:
         if isinstance(copy, tuple):
 
-            @pl.when(copy[0] != g)
+            @pl.when(copy[0])
             def _(copy=copy):
                 copy[1].wait_send()
 
@@ -509,7 +546,6 @@
     head_width = head_count * value_up.shape[2]
     block = out_proj.shape[1]
     width, units = 2 * block, down.shape[0]
-    band = owners * rows
     vmem, anywhere = pl.BlockSpec(memory_space=pltpu.VMEM), pl.BlockSpec(memory_space=pl.ANY)
     smem, dma = pl.BlockSpec(memory_space=pltpu.SMEM), pltpu.SemaphoreType.DMA
     return pl.pallas_call(
@@ -526,33 +562,33 @@
             pltpu.VMEM((nep, rows, head_width), BF),
             pltpu.VMEM((owners, rows, block), BF),
             pltpu.VMEM((nep, rows, 128), F32),
-            pltpu.VMEM((ng, band, block), F32),
-            pltpu.VMEM((ng, band, block), BF),
-            pltpu.VMEM((ng, band, block), BF),
-            pltpu.VMEM((nz, band, block), BF),
-            pltpu.VMEM((band, 128), F32),
-            pltpu.VMEM((2, ng, band, 128), F32),
-            pltpu.VMEM((2, ng, band, block), BF),
-            pltpu.VMEM((ng, nep * rows, 2 * units), BF),
-            pltpu.VMEM((ng, nep * rows, 2 * units), BF),
-            pltpu.VMEM((ng, nep * rows, units), BF),
-            pltpu.VMEM((2, nz, 2, rows, block), BF),
+            pltpu.VMEM((2, ng, rows, block), F32),
+            pltpu.VMEM((2, ng, rows, block), BF),
+            pltpu.VMEM((2, ng, rows, block), BF),
+            pltpu.VMEM((2, nz, rows, block), BF),
+            pltpu.VMEM((2, rows, 128), F32),
+            pltpu.VMEM((2, 2, ng, rows, 128), F32),
+            pltpu.VMEM((2, 2, ng, rows, block), BF),
+            pltpu.VMEM((2, ng, nz * rows, 2 * units), BF),
+            pltpu.VMEM((2, ng, nz * rows, 2 * units), BF),
+            pltpu.VMEM((2, ng, nz * rows, units), BF),
+            pltpu.VMEM((2, 2, nz, rows, block), BF),
             pltpu.VMEM((2, nz, rows, block), BF),
             pltpu.VMEM((2, nz, rows, block), BF),
             pltpu.VMEM((2, nz, rows, block), BF),
             pltpu.VMEM((2, ng, rows, block), BF),
             dma((8 + ng,)),
-            dma((96,)),
+            dma((128,)),
             dma((nep,)),
             dma((owners,)),
             dma((nep,)),
-            dma((ng,)),
-            dma((nz,)),
             dma((2, ng)),
+            dma((2, nz)),
+            dma((2, 2, ng)),
+            dma((2, 2, ng)),
             dma((2, ng)),
             dma((ng,)),
-            dma((ng,)),
-            dma((ng,)),
+            dma((2, ng)),
             dma((2,)),
             dma((2, nz)),
             dma((2, ng)),
@@ -607,7 +643,7 @@
         2 * expert_ids.shape[2] == nep
         and nep == 2 * ng
         and feature_count % (nep * 128) == 0
-        and micro * row_local % 16 == 0
+        and micro * row_local == 16
         and down_proj.shape[1] == 128
         and ng % 2 == 0
     )

time: 68.1 us -> 64.8 us (0.952); the launches traced: 67.1 us -> 64.7 us
  Pallas kernels: 65.5 us -> 63 us
    pallas_call x1, Pallas kernels: 65.5 us -> 63 us  [fused_layer(): pl.pallas_call(functools.partial(layer_kernel, ng, nep), out_shape=jax.Sh...]
where the time goes in v4:
time: 64.8 us; the launch traced here: 64.7 us
  Pallas kernels  63 us (97%)
  local copies, waits for them, and re-layouts  1.64 us (3%)
    pallas_call x1, Pallas kernels, fused_layer(): pl.pallas_call(functools.partial(layer_kernel, ng, nep), out_shape=jax.Sh...  63 us
    unnamed x1, local copies, waits for them, and re-layouts  1.64 us

profile of v4, /device:TPU:1, one launch (start us, length us, event | category | flops | bytes accessed | tf_op | source)
XLA Modules:
  0.0 64.7 jit_solution(16089661029361162919)
XLA Ops:
  0.0 63.0 %shard_map.109 = bf16[16,7168]{1,0:T(8,128)(2,1)} custom-call(s32[2,8]{1,0:T(2,128)} %len_ref.1, bf16[16,16,576]{2,1,0:T(8,128)(2,1)} %bitcast.15, bf16[16,7168]{1,0:T(8,128)(2,1)} %bitcast.16, s32[2,4,8]{2,1,0:T(4,128)} %bitcast.18, f32[2,4,8]{2,1,0:T(4,128)} %bitcast.19, f32[8,1,896]{2,1,0:T(1,128)} %bitcast.17, bf16[16,576,256]{2,1,0:T(8,128)(2,1)} %bitcast.11, ...), custom_call_target="tpu_custom_call" | custom-call | tf_op jit(solution)/shard_map/pallas_call | solution.py:551
  63.0 1.6 %copy.13 = bf16[2,8,7168]{2,1,0:T(8,128)(2,1)} copy(bf16[2,8,7168]{2,1,0:T(8,128)(2,1)} %bitcast.14) | data formatting | bytes 458752

commit v5 on v4

--- a/solution.py
+++ b/solution.py
@@ -175,6 +175,7 @@
     vu,
     wo,
     gu,
+    gate_up,
     dn,
     heads,
     hid_blk,
@@ -279,6 +280,37 @@
     def arrived(dst, recv):
         remote(dst, dst, recv, sibling, 0).wait_recv()
 
+    lane = lax.broadcasted_iota(jnp.int32, (1, 128), 1)
+    micro, top_count, row_local = id_ref.shape
+    for r in range(rows):
+        row = jnp.zeros((1, 128), F32)
+        for k in range(top_count):
+            m, i = r // row_local, r % row_local
+            row = row + jnp.where(lane == id_ref[m, k, i], gate_ref[m, k, i], 0.0)
+        coefs[j, r : r + 1, :] = row
+    for peer in ep_peers:
+        send(coefs.at[j], coefs.at[j], coef_sem.at[j], peer)
+
+    is_source = j // owners == g
+    hid_sends = []
+    for k, peer in enumerate(ep_peers):
+        start = pl.multiple_of(peer[1] * block, 128)
+        hid_sends.append(
+            remote(
+                hid_ref.at[:, pl.ds(start, block)],
+                hid_blk.at[j % owners],
+                hid_sem.at[j % owners],
+                peer,
+                send_sem.shape[0] - nep + k,
+            )
+        )
+
+    @pl.when(is_source)
+    def _():
+        for copy in hid_sends:
+            copy.start()
+        hid_blk[j % owners] = hid_ref[:, pl.ds(pl.multiple_of(j * block, 128), block)]
+
     for peer in g_peers:
         start = pl.multiple_of(peer[0] * slice_width, 128)
         send(dn_hbm.at[:, pl.ds(start, slice_width)], dn.at[g], dn_sem.at[g], peer)
@@ -299,36 +331,21 @@
     for d in range(1, nz):
         send(heads.at[j], heads.at[j], heads_sem.at[j], (g, (z + d) % nz * 2 + c))
     send(heads.at[j], heads.at[j], heads_sem.at[j], sibling)
-    lane = lax.broadcasted_iota(jnp.int32, (1, 128), 1)
-    micro, top_count, row_local = id_ref.shape
-    for r in range(rows):
-        row = jnp.zeros((1, 128), F32)
-        for k in range(top_count):
-            m, i = r // row_local, r % row_local
-            row = row + jnp.where(lane == id_ref[m, k, i], gate_ref[m, k, i], 0.0)
-        coefs[j, r : r + 1, :] = row
-    for peer in ep_peers:
-        send(coefs.at[j], coefs.at[j], coef_sem.at[j], peer)
-
-    is_source = j // owners == g
-    hid_sends = []
-    for k, peer in enumerate(ep_peers):
-        start = pl.multiple_of(peer[1] * block, 128)
-        hid_sends.append(
-            remote(
-                hid_ref.at[:, pl.ds(start, block)],
-                hid_blk.at[j % owners],
-                hid_sem.at[j % owners],
-                peer,
-                send_sem.shape[0] - nep + k,
-            )
-        )
-
-    @pl.when(is_source)
-    def _():
-        for copy in hid_sends:
-            copy.start()
-        hid_blk[j % owners] = hid_ref[:, pl.ds(pl.multiple_of(j * block, 128), block)]
+    for load in gu_loads:
+        load.wait()
+    to = lax.broadcasted_iota(jnp.int32, (256, 256), 0)
+    source = lax.broadcasted_iota(jnp.int32, (256, 256), 1)
+    wanted = jnp.where(to < 128, 2 * to, 2 * (to - 128) + 1)
+    order = jnp.where(source == wanted, 1.0, 0.0).astype(BF)
+    mixed = gu.reshape(ng, 2 * gu.shape[1], 128)
+    for t in range(gu.shape[1] // 128):
+        lines = jnp.concatenate([mixed[s, t * 256 : (t + 1) * 256, :] for s in range(ng)], axis=1)
+        sorted_lines = jnp.dot(order, lines, preferred_element_type=F32).astype(BF)
+        for s in range(ng):
+            for i in range(2):
+                gate_up[t * 128 : (t + 1) * 128, s * 256 + i * 128 : s * 256 + (i + 1) * 128] = (
+                    sorted_lines[i * 128 : (i + 1) * 128, s * 128 : (s + 1) * 128]
+                )
 
     for d in range(1, nz):
         slot = (z + d) % nz * 2 + c
@@ -404,35 +421,12 @@
         pieces = []
         for b in range(2):
             rows_in = res[h, b].reshape(count, block).astype(F32)
-            normed = (rows_in * scale * gain_ref[2 * g + b]).astype(BF)
-            pieces += [normed[:, i : i + 128] for i in range(0, block, 128)]
-        feature = lax.broadcasted_iota(jnp.int32, (128, 512), 0)
-        place = lax.broadcasted_iota(jnp.int32, (128, 512), 1)
-        wanted = jnp.where(place < 256, 2 * feature, 256 + 2 * feature + 1)
-        spacing = jnp.where(place == wanted, 1.0, 0.0).astype(BF)
-        spaced = jnp.dot(
-            jnp.concatenate(pieces, axis=0), spacing, preferred_element_type=F32
+            pieces.append((rows_in * scale * gain_ref[2 * g + b]).astype(BF))
+        pre = jnp.dot(
+            jnp.concatenate(pieces, axis=1), gate_up[...], preferred_element_type=F32
         ).astype(BF)
-        features = jnp.concatenate(
-            [
-                jnp.concatenate(
-                    [
-                        spaced[i * count : (i + 1) * count, :256],
-                        spaced[i * count : (i + 1) * count, 256:],
-                    ],
-                    axis=0,
-                )
-                for i in range(len(pieces))
-            ],
-            axis=1,
-        )
-        mixed = gu.reshape(ng, 2 * gu.shape[1], 128)
-        for s in range(0, ng, 2):
-            columns = jnp.concatenate([mixed[s], mixed[s + 1]], axis=1)
-            pre = jnp.dot(features, columns, preferred_element_type=F32).astype(BF)
-            for i in range(2):
-                pre_send[h, s + i, :, :units] = pre[:count, i * 128 : (i + 1) * 128]
-                pre_send[h, s + i, :, units:] = pre[count:, i * 128 : (i + 1) * 128]
+        for s in range(ng):
+            pre_send[h, s] = pre[:, s * 2 * units : (s + 1) * 2 * units]
         for peer in g_peers:
             send(pre_send.at[h, peer[0]], pre_rx.at[h, g], pre_sem.at[h, g], peer)
 
@@ -478,8 +472,6 @@
         spread_blocks(h)
     for h in range(2):
         share_blocks(h)
-    for load in gu_loads:
-        load.wait()
     for h in range(2):
         pre_activate(h)
     for h in range(2):
@@ -558,6 +550,7 @@
             pltpu.VMEM(value_up.shape, BF),
             pltpu.VMEM(out_proj.shape, BF),
             pltpu.VMEM((ng, gate_up.shape[0], 2, 128), BF),
+            pltpu.VMEM((gate_up.shape[0], ng * 256), BF),
             pltpu.VMEM((ng, units, width), BF),
             pltpu.VMEM((nep, rows, head_width), BF),
             pltpu.VMEM((owners, rows, block), BF),
@@ -594,7 +587,7 @@
             dma((2, ng)),
         ],
         compiler_params=pltpu.CompilerParams(
-            collective_id=0, has_side_effects=True, vmem_limit_bytes=60 * 1024 * 1024
+            collective_id=0, has_side_effects=True, vmem_limit_bytes=52 * 1024 * 1024
         ),
     )(lengths, queries, hidden, ids, gates, gain, cache, value_up, out_proj, gate_up, down)
 

time: 64.8 us -> 66.2 us (1.022)
  local copies, waits for them, and re-layouts: 1.64 us -> 5.4 us
  Pallas kernels: 63 us -> 60.4 us
    unnamed x1 -> x13, local copies, waits for them, and re-layouts: 1.64 us -> 5.4 us
    pallas_call x1, Pallas kernels: 63 us -> 60.4 us  [fused_layer(): pl.pallas_call(functools.partial(layer_kernel, ng, nep), out_shape=jax.Sh...]
where the time goes in v5:
time: 66.2 us; the launch traced here: 65.8 us
  Pallas kernels  60.4 us (91%)
  local copies, waits for them, and re-layouts  5.4 us (8%)
    pallas_call x1, Pallas kernels, fused_layer(): pl.pallas_call(functools.partial(layer_kernel, ng, nep), out_shape=jax.Sh...  60.4 us
    unnamed x13, local copies, waits for them, and re-layouts  5.4 us

profile of v5, /device:TPU:1, one launch (start us, length us, event | category | flops | bytes accessed | tf_op | source)
XLA Modules:
  0.0 65.8 jit_solution(3656928332259017742)
XLA Ops:
  0.0 0.0 copy-start
  0.0 1.0 %copy-done = bf16[2,8,16,576]{3,2,1,0:T(8,128)(2,1)S(1)} copy-done((bf16[2,8,16,576]{3,2,1,0:T(8,128)(2,1)S(1)}, bf16[2,8,16,576]{3,2,1,0:T(8,128)(2,1)}, u32[]{:S(2)}) %copy-start) | copy-done | bytes 294936
  1.0 0.0 copy-start.1
  1.0 0.9 %copy-done.1 = bf16[2,8,7168]{2,1,0:T(8,128)(2,1)S(1)} copy-done((bf16[2,8,7168]{2,1,0:T(8,128)(2,1)S(1)}, bf16[2,8,7168]{2,1,0:T(8,128)(2,1)}, u32[]{:S(2)}) %copy-start.1) | copy-done | bytes 229400
  1.9 0.0 copy-start.2
  1.9 0.7 %copy-done.2 = f32[7168]{0:T(1024)S(1)} copy-done((f32[7168]{0:T(1024)S(1)}, f32[7168]{0:T(1024)}, u32[]{:S(2)}) %copy-start.2) | copy-done | bytes 28696
  2.7 0.0 copy-start.3
  2.7 0.7 %copy-done.3 = s32[2,8,4]{1,2,0:T(4,128)S(1)} copy-done((s32[2,8,4]{1,2,0:T(4,128)S(1)}, s32[2,8,4]{1,2,0:T(4,128)}, u32[]{:S(2)}) %copy-start.3) | copy-done | bytes 280
  3.3 0.0 copy-start.4
  3.4 0.7 %copy-done.4 = f32[2,8,4]{1,2,0:T(4,128)S(1)} copy-done((f32[2,8,4]{1,2,0:T(4,128)S(1)}, f32[2,8,4]{1,2,0:T(4,128)}, u32[]{:S(2)}) %copy-start.4) | copy-done | bytes 280
  4.0 0.0 copy-start.5
  4.0 0.7 %copy-done.5 = s32[2,8]{1,0:T(2,128)S(1)} copy-done((s32[2,8]{1,0:T(2,128)S(1)}, s32[2,8]{1,0:T(2,128)}, u32[]{:S(2)}) %copy-start.5) | copy-done | bytes 88
  4.7 60.4 %shard_map.109 = bf16[16,7168]{1,0:T(8,128)(2,1)S(1)} custom-call(s32[2,8]{1,0:T(2,128)S(1)} %copy-done.5, bf16[16,16,576]{2,1,0:T(8,128)(2,1)S(1)} %bitcast.12, bf16[16,7168]{1,0:T(8,128)(2,1)S(1)} %bitcast.13, s32[2,4,8]{2,1,0:T(4,128)S(1)} %bitcast.15, f32[2,4,8]{2,1,0:T(4,128)S(1)} %bitcast.16, f32[8,1,896]{2,1,0:T(1,128)S(1)} %bitcast.14, ...), custom_call_target="tpu_custom_call" | custom-call | tf_op jit(solution)/shard_map/pallas_call | solution.py:543
  65.1 0.7 %copy.13 = bf16[2,8,7168]{2,1,0:T(8,128)(2,1)} copy(bf16[2,8,7168]{2,1,0:T(8,128)(2,1)S(1)} %bitcast.11) | data formatting | bytes 458752
Async XLA Ops:
  0.0 1.0 %copy-start = (bf16[2,8,16,576]{3,2,1,0:T(8,128)(2,1)S(1)}, bf16[2,8,16,576]{3,2,1,0:T(8,128)(2,1)}, u32[]{:S(2)}) copy-start(bf16[2,8,16,576]{3,2,1,0:T(8,128)(2,1)} %param.12) | copy-start | bytes 884740
  1.0 0.9 %copy-start.1 = (bf16[2,8,7168]{2,1,0:T(8,128)(2,1)S(1)}, bf16[2,8,7168]{2,1,0:T(8,128)(2,1)}, u32[]{:S(2)}) copy-start(bf16[2,8,7168]{2,1,0:T(8,128)(2,1)} %param.11) | copy-start | bytes 688132
  1.9 0.7 %copy-start.2 = (f32[7168]{0:T(1024)S(1)}, f32[7168]{0:T(1024)}, u32[]{:S(2)}) copy-start(f32[7168]{0:T(1024)} %param.17) | copy-start | bytes 86020
  2.7 0.7 %copy-start.3 = (s32[2,8,4]{1,2,0:T(4,128)S(1)}, s32[2,8,4]{1,2,0:T(4,128)}, u32[]{:S(2)}) copy-start(s32[2,8,4]{1,2,0:T(4,128)} %param.15) | copy-start | bytes 772
  3.3 0.7 %copy-start.4 = (f32[2,8,4]{1,2,0:T(4,128)S(1)}, f32[2,8,4]{1,2,0:T(4,128)}, u32[]{:S(2)}) copy-start(f32[2,8,4]{1,2,0:T(4,128)} %param.16) | copy-start | bytes 772
  4.0 0.7 %copy-start.5 = (s32[2,8]{1,0:T(2,128)S(1)}, s32[2,8]{1,0:T(2,128)}, u32[]{:S(2)}) copy-start(s32[2,8]{1,0:T(2,128)} %len_ref.1) | copy-start | bytes 196

commit v6 on v5

--- a/solution.py
+++ b/solution.py
@@ -143,34 +143,33 @@
         masked.append(jnp.where(in_range, scores, -1e30))
     masked = jnp.concatenate(masked, axis=0)
     exponent = jnp.exp(masked - jnp.max(masked, axis=1, keepdims=True))
-    weights = (exponent / jnp.sum(exponent, axis=1, keepdims=True)).astype(BF)
-    latents = [
-        lax.dot_general(
-            weights[r * head_count : (r + 1) * head_count],
-            cache[r, :latent_width, :],
-            (((1,), (1,)), ((), ())),
-            preferred_element_type=F32,
-        ).astype(BF)
-        for r in range(rows)
-    ]
-    return jnp.concatenate(latents, axis=0)
+    weights = exponent / jnp.sum(exponent, axis=1, keepdims=True)
+    turned = jnp.transpose(weights).astype(BF)
+    column = lax.broadcasted_iota(jnp.int32, (latent_width, rows * head_count), 1)
+    latents = jnp.zeros((latent_width, rows * head_count), F32)
+    for r in range(rows):
+        mixed = jnp.dot(cache[r, :latent_width, :], turned, preferred_element_type=F32)
+        latents = jnp.where(column // head_count == r, mixed, latents)
+    return latents.astype(BF)
 
 
 def layer_kernel(
     ng,
     nep,
     len_ref,
-    q_ref,
-    hid_ref,
+    q_hbm,
+    hid_hbm,
     id_ref,
     gate_ref,
-    gain_ref,
+    gain_hbm,
     cache_hbm,
     vu_hbm,
     wo_hbm,
     gu_hbm,
     dn_hbm,
     out_ref,
+    q_ref,
+    gain_ref,
     cache,
     vu,
     wo,
@@ -241,7 +240,9 @@
     ]
     own_slice = pl.ds(pl.multiple_of(g * slice_width, 128), slice_width)
     dn_load = pltpu.make_async_copy(dn_hbm.at[:, own_slice], dn.at[g], load_sem.at[7])
-    for load in cache_loads + [vu_load, wo_load, dn_load] + gu_loads:
+    q_load = pltpu.make_async_copy(q_hbm, q_ref, load_sem.at[8 + ng])
+    gain_load = pltpu.make_async_copy(gain_hbm, gain_ref, load_sem.at[9 + ng])
+    for load in [q_load] + cache_loads + [vu_load, gain_load, wo_load, dn_load] + gu_loads:
         load.start()
 
     barrier = pltpu.get_barrier_semaphore()
@@ -297,7 +298,7 @@
         start = pl.multiple_of(peer[1] * block, 128)
         hid_sends.append(
             remote(
-                hid_ref.at[:, pl.ds(start, block)],
+                hid_hbm.at[:, pl.ds(start, block)],
                 hid_blk.at[j % owners],
                 hid_sem.at[j % owners],
                 peer,
@@ -305,23 +306,33 @@
             )
         )
 
+    hid_load = pltpu.make_async_copy(
+        hid_hbm.at[:, pl.ds(pl.multiple_of(j * block, 128), block)],
+        hid_blk.at[j % owners],
+        load_sem.at[2],
+    )
+
     @pl.when(is_source)
     def _():
         for copy in hid_sends:
             copy.start()
-        hid_blk[j % owners] = hid_ref[:, pl.ds(pl.multiple_of(j * block, 128), block)]
+        hid_load.start()
+        hid_load.wait()
 
     for peer in g_peers:
         start = pl.multiple_of(peer[0] * slice_width, 128)
         send(dn_hbm.at[:, pl.ds(start, slice_width)], dn.at[g], dn_sem.at[g], peer)
 
+    q_load.wait()
     latents = attend_rows(len_ref, q_ref, cache, cache_loads, vu.shape[1])
     vu_load.wait()
     count = rows * head_count
     to = lax.broadcasted_iota(jnp.int32, (count, count), 0)
     source = lax.broadcasted_iota(jnp.int32, (count, count), 1)
     swap = jnp.where(source == to % rows * head_count + to // rows, 1.0, 0.0).astype(BF)
-    by_head = jnp.dot(swap, latents, preferred_element_type=F32).astype(BF)
+    by_head = lax.dot_general(
+        swap, latents, (((1,), (1,)), ((), ())), preferred_element_type=F32
+    ).astype(BF)
     value_width = vu.shape[2]
     for h in range(head_count):
         heads[j, :, h * value_width : (h + 1) * value_width] = jnp.dot(
@@ -464,6 +475,7 @@
                     copy.start()
 
     wo_load.wait()
+    gain_load.wait()
     for h in range(2):
         project(h)
     for h in range(2):
@@ -543,9 +555,11 @@
     return pl.pallas_call(
         functools.partial(layer_kernel, ng, nep),
         out_shape=jax.ShapeDtypeStruct((rows, nep * block), BF),
-        in_specs=[smem, vmem, vmem, smem, smem, vmem] + [anywhere] * 5,
+        in_specs=[smem, anywhere, anywhere, smem, smem] + [anywhere] * 6,
         out_specs=vmem,
         scratch_shapes=[
+            pltpu.VMEM(queries.shape, BF),
+            pltpu.VMEM(gain.shape, F32),
             pltpu.VMEM(cache.shape, BF),
             pltpu.VMEM(value_up.shape, BF),
             pltpu.VMEM(out_proj.shape, BF),
@@ -570,7 +584,7 @@
             pltpu.VMEM((2, nz, rows, block), BF),
             pltpu.VMEM((2, nz, rows, block), BF),
             pltpu.VMEM((2, ng, rows, block), BF),
-            dma((8 + ng,)),
+            dma((10 + ng,)),
             dma((128,)),
             dma((nep,)),
             dma((owners,)),
@@ -587,7 +601,7 @@
             dma((2, ng)),
         ],
         compiler_params=pltpu.CompilerParams(
-            collective_id=0, has_side_effects=True, vmem_limit_bytes=52 * 1024 * 1024
+            collective_id=0, has_side_effects=True, vmem_limit_bytes=60 * 1024 * 1024
         ),
     )(lengths, queries, hidden, ids, gates, gain, cache, value_up, out_proj, gate_up, down)
 

time: 66.2 us -> 66.6 us (level)
  local copies, waits for them, and re-layouts: 5.4 us -> 1.64 us
  Pallas kernels: 60.4 us -> 64.1 us
    unnamed x13 -> x1, local copies, waits for them, and re-layouts: 5.4 us -> 1.64 us
    pallas_call x1, Pallas kernels: 60.4 us -> 64.1 us  [fused_layer(): pl.pallas_call(functools.partial(layer_kernel, ng, nep), out_shape=jax.Sh...]
where the time goes in v6:
time: 66.6 us; the launch traced here: 65.7 us
  Pallas kernels  64.1 us (96%)
  local copies, waits for them, and re-layouts  1.64 us (2%)
    pallas_call x1, Pallas kernels, fused_layer(): pl.pallas_call(functools.partial(layer_kernel, ng, nep), out_shape=jax.Sh...  64.1 us
    unnamed x1, local copies, waits for them, and re-layouts  1.64 us

profile of v6, /device:TPU:1, one launch (start us, length us, event | category | flops | bytes accessed | tf_op | source)
XLA Modules:
  0.0 65.7 jit_solution(8012558817195724920)
XLA Ops:
  0.0 64.1 %shard_map.109 = bf16[16,7168]{1,0:T(8,128)(2,1)} custom-call(s32[2,8]{1,0:T(2,128)} %len_ref.1, bf16[16,16,576]{2,1,0:T(8,128)(2,1)} %bitcast.15, bf16[16,7168]{1,0:T(8,128)(2,1)} %bitcast.16, s32[2,4,8]{2,1,0:T(4,128)} %bitcast.18, f32[2,4,8]{2,1,0:T(4,128)} %bitcast.19, f32[8,1,896]{2,1,0:T(1,128)} %bitcast.17, bf16[16,576,256]{2,1,0:T(8,128)(2,1)} %bitcast.11, ...), custom_call_target="tpu_custom_call" | custom-call | tf_op jit(solution)/shard_map/pallas_call | solution.py:555
  64.1 1.6 %copy.13 = bf16[2,8,7168]{2,1,0:T(8,128)(2,1)} copy(bf16[2,8,7168]{2,1,0:T(8,128)(2,1)} %bitcast.14) | data formatting | bytes 458752

commit v7 on v6

--- a/solution.py
+++ b/solution.py
@@ -143,14 +143,17 @@
         masked.append(jnp.where(in_range, scores, -1e30))
     masked = jnp.concatenate(masked, axis=0)
     exponent = jnp.exp(masked - jnp.max(masked, axis=1, keepdims=True))
-    weights = exponent / jnp.sum(exponent, axis=1, keepdims=True)
-    turned = jnp.transpose(weights).astype(BF)
-    column = lax.broadcasted_iota(jnp.int32, (latent_width, rows * head_count), 1)
-    latents = jnp.zeros((latent_width, rows * head_count), F32)
-    for r in range(rows):
-        mixed = jnp.dot(cache[r, :latent_width, :], turned, preferred_element_type=F32)
-        latents = jnp.where(column // head_count == r, mixed, latents)
-    return latents.astype(BF)
+    weights = (exponent / jnp.sum(exponent, axis=1, keepdims=True)).astype(BF)
+    latents = [
+        lax.dot_general(
+            weights[r * head_count : (r + 1) * head_count],
+            cache[r, :latent_width, :],
+            (((1,), (1,)), ((), ())),
+            preferred_element_type=F32,
+        ).astype(BF)
+        for r in range(rows)
+    ]
+    return jnp.concatenate(latents, axis=0)
 
 
 def layer_kernel(
@@ -330,9 +333,7 @@
     to = lax.broadcasted_iota(jnp.int32, (count, count), 0)
     source = lax.broadcasted_iota(jnp.int32, (count, count), 1)
     swap = jnp.where(source == to % rows * head_count + to // rows, 1.0, 0.0).astype(BF)
-    by_head = lax.dot_general(
-        swap, latents, (((1,), (1,)), ((), ())), preferred_element_type=F32
-    ).astype(BF)
+    by_head = jnp.dot(swap, latents, preferred_element_type=F32).astype(BF)
     value_width = vu.shape[2]
     for h in range(head_count):
         heads[j, :, h * value_width : (h + 1) * value_width] = jnp.dot(

time: 66.6 us -> 66.2 us (level)
  no operation moved by 1% of the time
where the time goes in v7:
time: 66.2 us; the launch traced here: 65.7 us
  Pallas kernels  64 us (97%)
  local copies, waits for them, and re-layouts  1.64 us (2%)
    pallas_call x1, Pallas kernels, fused_layer(): pl.pallas_call(functools.partial(layer_kernel, ng, nep), out_shape=jax.Sh...  64 us
    unnamed x1, local copies, waits for them, and re-layouts  1.64 us

profile of v7, /device:TPU:1, one launch (start us, length us, event | category | flops | bytes accessed | tf_op | source)
XLA Modules:
  0.0 65.7 jit_solution(3811420319663941802)
XLA Ops:
  0.0 64.0 %shard_map.109 = bf16[16,7168]{1,0:T(8,128)(2,1)} custom-call(s32[2,8]{1,0:T(2,128)} %len_ref.1, bf16[16,16,576]{2,1,0:T(8,128)(2,1)} %bitcast.15, bf16[16,7168]{1,0:T(8,128)(2,1)} %bitcast.16, s32[2,4,8]{2,1,0:T(4,128)} %bitcast.18, f32[2,4,8]{2,1,0:T(4,128)} %bitcast.19, f32[8,1,896]{2,1,0:T(1,128)} %bitcast.17, bf16[16,576,256]{2,1,0:T(8,128)(2,1)} %bitcast.11, ...), custom_call_target="tpu_custom_call" | custom-call | tf_op jit(solution)/shard_map/pallas_call | solution.py:556
  64.0 1.6 %copy.13 = bf16[2,8,7168]{2,1,0:T(8,128)(2,1)} copy(bf16[2,8,7168]{2,1,0:T(8,128)(2,1)} %bitcast.14) | data formatting | bytes 458752
